TPU v7x, 32 devices: a whole 2x2x4 slice. The times are simulated.
32 devices in a mesh: sec: 4 (over y, core), proto: 8 (over z, x).
Axes of the slice: x: 2, y: 2, z: 4, core: 2. Of those that a mesh axis runs over, the one named last changes fastest.
Arguments:
- features: bfloat16 [2048, 512], P('sec'), may hold values from -700 to 700
- prototypes: bfloat16 [512, 262144], P(None, 'proto'), may hold values from -20 to 20
- crop_sample: int32 [2048], P('sec'), may hold values from 0 to 511, as said below
- crop_live: int32 [2048], P('sec'), may hold values 0 or 1
Outputs:
- crop_loss: float32 [2048], P('sec')
- embed_grad: float32 [2048, 512], P(('sec', 'proto'))
Inputs may be any that keep to these rules, and one draw needn't show every extreme that they name: `crop_sample`: on student rows the index of a teacher row, 0 to 511; the entries on teacher rows are not read.
All inputs are finite; a program needn't handle non-finite values. No bound on the sum of `crop_live` on one device may be relied on, other than what follows from the above.
Results may differ from a plain program's by a relative error of at most 0.0067.
Values may be sent and summed in bfloat16 or wider, within the bound.
A program may use at most 448 MiB of HBM per device.

v0:
```python
import jax
import jax.numpy as jnp
from jax import lax
from jax.sharding import PartitionSpec as P

PROTOS = 262144
ITERS = 3


TEACH_TEMP = 0.07
STUD_TEMP = 0.1


def from_root(block, axis, owner):
    block = jnp.where(lax.axis_index(axis) == owner, block, jnp.zeros_like(block))
    return lax.psum(block, axis)


def unit_rows_of(features):
    values = features.astype(jnp.float32)
    scaled = values * lax.rsqrt(jnp.sum(values * values, axis=1, keepdims=True) + 1e-06)
    return scaled.astype(jnp.bfloat16)


def per_device(features, prototypes, crop_sample, crop_live):
    row_count = features.shape[0]
    feat_width = features.shape[1]
    shard_cols = prototypes.shape[1]
    proto_devs = lax.axis_size("proto")
    teach_devs = lax.axis_size("sec") // 4
    first_dev = lax.axis_size("sec") // 2 - teach_devs // 2
    sample_count = row_count * teach_devs
    sec_index = lax.axis_index("sec")
    is_teacher = jnp.logical_and(sec_index >= first_dev, sec_index < first_dev + teach_devs)
    is_student = jnp.logical_not(is_teacher)
    unit_rows = unit_rows_of(features)
    logits = jnp.dot(unit_rows, prototypes, preferred_element_type=jnp.float32)
    teacher_logits = logits / TEACH_TEMP
    row_top = lax.pmax(jnp.max(teacher_logits, axis=1), "proto")
    expo_tab = lax.cond(
        is_teacher,
        lambda operand: jnp.exp(operand - row_top[:, None]),
        lambda operand: jnp.zeros_like(operand),
        teacher_logits,
    )
    row_weight = jnp.ones((row_count,), jnp.float32)
    col_scale = jnp.ones((shard_cols,), jnp.float32)
    for sweep in range(ITERS):
        col_part = jnp.dot(row_weight, expo_tab, precision=lax.Precision.HIGHEST)
        col_total = lax.psum(col_part, "sec")
        col_scale = 1.0 / (PROTOS * col_total)
        if sweep + 1 < ITERS:
            row_part = jnp.dot(expo_tab, col_scale, precision=lax.Precision.HIGHEST)
            row_total = lax.psum(row_part, "proto")
            safe_total = jnp.where(is_teacher, row_total, 1.0)
            row_weight = jnp.where(is_teacher, 1.0 / (sample_count * safe_total), 0.0)
    gathered = []
    for root_index in range(teach_devs):
        gathered.append(from_root(unit_rows, "sec", first_dev + root_index))
    sample_rows = jnp.concatenate(gathered, axis=0)
    crop_rows = jnp.take(sample_rows, crop_sample, axis=0)
    crop_logits = lax.cond(
        is_student,
        lambda operand: jnp.dot(operand, prototypes, preferred_element_type=jnp.float32)
        / TEACH_TEMP,
        lambda operand: jnp.zeros((row_count, shard_cols), jnp.float32),
        crop_rows,
    )
    stud_logits = logits / STUD_TEMP
    stud_top, crop_top = lax.pmax(
        (jnp.max(stud_logits, axis=1), jnp.max(crop_logits, axis=1)), "proto"
    )
    stud_exp = jnp.exp(stud_logits - stud_top[:, None])
    crop_exp = jnp.exp(crop_logits - crop_top[:, None]) * col_scale[None, :]
    stud_sum, crop_sum, cross_sum = lax.psum(
        (
            jnp.sum(stud_exp, axis=1),
            jnp.sum(crop_exp, axis=1),
            jnp.sum(crop_exp * stud_logits, axis=1),
        ),
        "proto",
    )
    log_total = stud_top + jnp.log(stud_sum)
    stud_probs = jnp.exp(stud_logits - log_total[:, None])
    target = crop_exp / crop_sum[:, None]
    weight = crop_live.astype(jnp.float32) * is_student.astype(jnp.float32)
    crop_loss = weight * (log_total - cross_sum / crop_sum)
    prob_gap = (weight[:, None] * (stud_probs - target)).astype(jnp.bfloat16)
    embed_grad = lax.psum_scatter(
        lax.cond(
            is_student,
            lambda operand: lax.dot_general(
                operand, prototypes, (((1,), (1,)), ((), ())), preferred_element_type=jnp.float32
            )
            / STUD_TEMP,
            lambda operand: jnp.zeros(
                (row_count // proto_devs * lax.axis_size("proto"), feat_width), jnp.float32
            ),
            prob_gap,
        ),
        "proto",
        scatter_dimension=0,
        tiled=True,
    )
    return (crop_loss, embed_grad)


def solution(mesh):
    in_specs = (P("sec", None), P(None, "proto"), P("sec"), P("sec"))
    out_specs = (P("sec"), P(("sec", "proto"), None))
    return jax.shard_map(
        per_device, mesh=mesh, in_specs=in_specs, out_specs=out_specs, check_vma=False
    )
```

profile of v0, /device:TPU:0, one launch (start us, length us, event | category | flops | bytes accessed | tf_op | source)
XLA Modules:
  0.0 753.9 jit_solution(11592569064051998402)
XLA Ops:
  10.6 56.2 %fusion.12 = (f32[512]{0:T(512)S(1)}, f32[512]{0:T(512)S(1)}, f32[512,32768]{1,0:T(8,128)}, f32[512,32768]{1,0:T(8,128)}) fusion(bf16[512,32768]{1,0:T(8,128)(2,1)} %param.11, bf16[512,512]{1,0:T(8,128)(2,1)} %param.10, f32[512]{0:T(512)S(1)} %add_rsqrt_fusion), kind=kOutput, calls=%fused_computation.36 | convolution fusion | flops 17247764480 | bytes 168302592 | tf_op jit(solution)/shard_map/dot_general | solution.py:37
  66.8 43.7 %conditional.3 = (f32[512,32768]{1,0:T(8,128)}) conditional(s32[]{:T(128)} %convert_element_type.26, () %tuple.37, (s32[512]{0:T(512)S(1)}, bf16[512,512]{1,0:T(8,128)(2,1)}, bf16[512,32768]{1,0:T(8,128)(2,1)}) %tuple.70), branch_computations={%region_6.0_spmd, %region_7.8_spmd.clone} | conditional | flops 17196914688 | bytes 102251528 | solution.py:62
  66.8 3.1 gather_fusion
  69.9 40.5 %convolution_multiply_fusion.1 = f32[512,32768]{1,0:T(8,128)} fusion(bf16[512,32768]{1,0:T(8,128)(2,1)} %get-tuple-element.85, bf16[512,512]{1,0:T(8,128)(2,1)S(1)} %gather_fusion, pred[512]{0:T(512)(128)(4,1)S(1)} %compare_and_fusion), kind=kOutput, calls=%fused_computation.3 | convolution fusion | flops 17196908544 | bytes 101188096 | tf_op jit(solution)/shard_map/cond/branch_1_fun/dot_general | solution.py:64
  110.4 20.7 %reduce_max.28 = f32[512]{0:T(512)S(1)} reduce(f32[512,32768]{1,0:T(8,128)} %get-tuple-element.106, f32[]{:T(128)} %constant.62.clone.1), dimensions={1}, to_apply=%region_8.9 | reduce | flops 16776704 | bytes 67110912 | tf_op jit(solution)/shard_map/reduce_max | solution.py:71
  131.1 23.9 %all-reduce.1 = (f32[512]{0:T(512)}, f32[512]{0:T(512)S(1)}, f32[512]{0:T(512)}) all-reduce(f32[512]{0:T(512)S(1)} %get-tuple-element.94, f32[512]{0:T(512)S(1)} %get-tuple-element.93, f32[512]{0:T(512)S(1)} %reduce_max.28), channel_id=1, replica_groups=mesh['sec'=4,'proto'=8] {'proto'}, use_global_device_ids=true, to_apply=%region_2.0 | all-reduce | flops 1536 | bytes 12288 | tf_op jit(solution)/shard_map/pmax | solution.py:70
  155.0 21.5 %conditional.4 = (f32[512,32768]{1,0:T(8,128)}) conditional(s32[]{:T(128)} %convert_element_type.27, () %tuple.39, (f32[512]{0:T(512)S(1)}, f32[512,32768]{1,0:T(8,128)}) %tuple.40), branch_computations={%region_12.13_spmd, %region_13.14_spmd} | conditional | flops 16777216 | bytes 134219776 | solution.py:40
  155.0 21.0 %broadcast.46 = f32[512,32768]{1,0:T(8,128)} broadcast(f32[]{:T(128)} %constant.53.clone), dimensions={} | broadcast | bytes 67108864 | tf_op jit(solution)/shard_map/broadcast.6
  176.5 38.2 %fusion.9 = f32[1,32768]{1,0:T(1,128)} fusion(f32[512,32768]{1,0:T(8,128)} %get-tuple-element.107), kind=kOutput, calls=%fused_computation.33 | convolution fusion | flops 201326592 | bytes 67239936 | tf_op jit(solution)/shard_map/dot_general | solution.py:49
  214.9 28.4 %all-reduce.9.cloned.1.call-done = f32[32768]{0:T(1024)} async-done(((f32[32768]{0:T(1024)}), f32[32768]{0:T(1024)}) %all-reduce.9.cloned.1.call-update) | async-done | bytes 131088 | tf_op jit(solution)/shard_map/psum | solution.py:50
  244.3 60.4 %fusion.13 = f32[1,512]{1,0:T(1,128)S(1)} fusion(f32[512,32768]{1,0:T(8,128)} %get-tuple-element.107, f32[32768,1]{0,1:T(1,128)S(1)} %bitcast.26), kind=kOutput, calls=%fused_computation.37 | convolution fusion | flops 201326592 | bytes 67241984 | tf_op jit(solution)/shard_map/dot_general | solution.py:53
  304.7 21.6 %psum.66 = f32[512]{0:T(512)S(1)} all-reduce(f32[512]{0:T(512)S(1)} %bitcast.29), channel_id=1, replica_groups=mesh['sec'=4,'proto'=8] {'proto'}, use_global_device_ids=true, to_apply=%region_15.16 | all-reduce | flops 512 | bytes 4096 | tf_op jit(solution)/shard_map/psum | solution.py:54
  326.3 38.2 %fusion.14 = f32[1,32768]{1,0:T(1,128)} fusion(f32[512,1]{0,1:T(1,128)S(1)} %bitcast.30, f32[512,32768]{1,0:T(8,128)} %get-tuple-element.107), kind=kOutput, calls=%fused_computation.38 | convolution fusion | flops 201326592 | bytes 67241984 | tf_op jit(solution)/shard_map/dot_general | solution.py:49
  364.8 27.5 %all-reduce.11.cloned.1.call-done = f32[32768]{0:T(1024)} async-done(((f32[32768]{0:T(1024)}), f32[32768]{0:T(1024)}) %all-reduce.11.cloned.1.call-update) | async-done | bytes 131088 | tf_op jit(solution)/shard_map/psum | solution.py:50
  393.2 60.4 %fusion.15 = f32[1,512]{1,0:T(1,128)S(1)} fusion(f32[512,32768]{1,0:T(8,128)} %get-tuple-element.107, f32[32768,1]{0,1:T(1,128)S(1)} %bitcast.27), kind=kOutput, calls=%fused_computation.39 | convolution fusion | flops 201326592 | bytes 67241984 | tf_op jit(solution)/shard_map/dot_general | solution.py:53
  453.6 21.6 %psum.68 = f32[512]{0:T(512)S(1)} all-reduce(f32[512]{0:T(512)S(1)} %bitcast.31), channel_id=1, replica_groups=mesh['sec'=4,'proto'=8] {'proto'}, use_global_device_ids=true, to_apply=%region_17.18 | all-reduce | flops 512 | bytes 4096 | tf_op jit(solution)/shard_map/psum | solution.py:54
  475.2 38.2 %fusion.16 = f32[1,32768]{1,0:T(1,128)} fusion(f32[512,1]{0,1:T(1,128)S(1)} %bitcast.28, f32[512,32768]{1,0:T(8,128)} %get-tuple-element.107), kind=kOutput, calls=%fused_computation.40 | convolution fusion | flops 201326592 | bytes 67241984 | tf_op jit(solution)/shard_map/dot_general | solution.py:49
  513.5 27.7 %all-reduce.13.cloned.1.call-done = f32[32768]{0:T(1024)} async-done(((f32[32768]{0:T(1024)}), f32[32768]{0:T(1024)}) %all-reduce.13.cloned.1.call-update) | async-done | bytes 131088 | tf_op jit(solution)/shard_map/psum | solution.py:50
  542.2 42.3 %fusion.4 = (f32[512]{0:T(512)S(1)}, f32[512]{0:T(512)S(1)}, f32[512]{0:T(512)S(1)}) fusion(f32[512,32768]{1,0:T(8,128)} %get-tuple-element.106, f32[32768]{0:T(1024)S(1)} %multiply_divide_fusion, f32[512]{0:T(512)S(1)} %copy-done.2, f32[512,32768]{1,0:T(8,128)} %get-tuple-element.105, f32[512]{0:T(512)S(1)} %copy-done.3), kind=kLoop, calls=%fused_computation.16 | loop fusion | flops 134216192 | bytes 134359040 | tf_op jit(solution)/shard_map/reduce_sum | solution.py:78
  584.5 21.6 %all-reduce = (f32[512]{0:T(512)S(1)}, f32[512]{0:T(512)S(1)}, f32[512]{0:T(512)S(1)}) all-reduce(f32[512]{0:T(512)S(1)} %get-tuple-element.92, f32[512]{0:T(512)S(1)} %get-tuple-element.91, f32[512]{0:T(512)S(1)} %get-tuple-element.90), channel_id=1, replica_groups=mesh['sec'=4,'proto'=8] {'proto'}, use_global_device_ids=true, to_apply=%region_4.0 | all-reduce | flops 1536 | bytes 12288 | tf_op jit(solution)/shard_map/psum | solution.py:75
  606.7 53.1 %multiply_convert_fusion = bf16[512,32768]{1,0:T(8,128)(2,1)} fusion(f32[512,32768]{1,0:T(8,128)} %get-tuple-element.105, f32[512,32768]{1,0:T(8,128)} %get-tuple-element.106, f32[512]{0:T(512)S(1)} %get-tuple-element.97, f32[512]{0:T(512)S(1)} %get-tuple-element.102, f32[512]{0:T(512)S(1)} %get-tuple-element.103, f32[32768]{0:T(1024)S(1)} %multiply_divide_fusion, ...), kind=kLoop, calls=%fused_computation.11 | loop fusion | flops 134217728 | bytes 167911424 | tf_op jit(solution)/shard_map/convert_element_type | solution.py:88
  659.8 26.0 %conditional.5 = (f32[512,512]{1,0:T(8,128)S(1)}) conditional(s32[]{:T(128)} %convert_element_type.26, () %tuple.41, (bf16[512,32768]{1,0:T(8,128)(2,1)}, bf16[512,32768]{1,0:T(8,128)(2,1)}) %tuple.42), branch_computations={%region_23.24_spmd, %region_24.25_spmd} | conditional | flops 17180131328 | bytes 68157448 | solution.py:90
  660.1 25.7 %convolution_multiply_fusion = f32[512,512]{1,0:T(8,128)S(1)} fusion(bf16[512,32768]{1,0:T(8,128)(2,1)} %get-tuple-element.77, bf16[512,32768]{1,0:T(8,128)(2,1)} %get-tuple-element.78), kind=kOutput, calls=%fused_computation.2 | convolution fusion | flops 17180131328 | bytes 68157440 | tf_op jit(solution)/shard_map/cond/branch_1_fun/dot_general | solution.py:92
  686.8 59.9 %reduce-scatter.2.cloned.1.call-done = f32[64,512]{1,0:T(8,128)} async-done(((f32[512,512]{1,0:T(8,128)}), f32[64,512]{1,0:T(8,128)}) %reduce-scatter.2.cloned.1.call-update) | async-done | bytes 131088 | tf_op jit(solution)/shard_map/reduce_scatter | solution.py:89
  (33 shorter events, 8.4 us)
Async XLA Ops:
  7.2 59.6 %all-reduce.7.cloned.1.call-start = ((), (), s32[]{:S(2)}) async-start(), calls=%async_computation.1 | async-start | bytes 1048576 | tf_op jit(solution)/shard_map/psum | solution.py:16
  10.5 56.3 %copy-start.1 = (s32[512]{0:T(512)S(1)}, s32[512]{0:T(512)}, u32[]{:S(2)}) copy-start(s32[512]{0:T(512)} %param.12) | copy-start | bytes 6148
  10.5 232.9 %all-reduce.9.cloned.1.call-start = ((), (), s32[]{:S(2)}) async-start(), calls=%async_computation.2 | async-start | bytes 262144 | tf_op jit(solution)/shard_map/psum | solution.py:50
  214.7 177.5 %all-reduce.11.cloned.1.call-start = ((), (), s32[]{:S(2)}) async-start(), calls=%async_computation.3 | async-start | bytes 262144 | tf_op jit(solution)/shard_map/psum | solution.py:50
  364.5 176.8 %all-reduce.13.cloned.1.call-start = ((), (), s32[]{:S(2)}) async-start(), calls=%async_computation.4 | async-start | bytes 262144 | tf_op jit(solution)/shard_map/psum | solution.py:50
  393.2 149.0 %copy-start.2 = (f32[512]{0:T(512)S(1)}, f32[512]{0:T(512)}, u32[]{:S(2)}) copy-start(f32[512]{0:T(512)} %get-tuple-element.100) | copy-start | bytes 6148
  393.2 149.0 %copy-start.3 = (f32[512]{0:T(512)S(1)}, f32[512]{0:T(512)}, u32[]{:S(2)}) copy-start(f32[512]{0:T(512)} %get-tuple-element.98) | copy-start | bytes 6148
  513.4 233.3 %reduce-scatter.2.cloned.1.call-start = ((), (), s32[]{:S(2)}) async-start(), calls=%async_computation.5 | async-start | bytes 1179648 | tf_op jit(solution)/shard_map/reduce_scatter | solution.py:89
  542.2 63.9 %copy-start.4 = (s32[512]{0:T(512)S(1)}, s32[512]{0:T(512)}, u32[]{:S(2)}) copy-start(s32[512]{0:T(512)} %param.13) | copy-start | bytes 6148
  685.8 1.0 copy-start
Sparse Core Ops, SparseCore 0:
  10.6 35.8 all-reduce.6
  214.8 28.4 all-reduce.8
  364.6 27.6 all-reduce.10
  513.6 27.6 all-reduce.12
  687.0 59.7 reduce-scatter.1
where the time goes:
time: 760 us; the launch traced here: 754 us
  matrix products  358 us (47%)
  waiting for transfers between devices  144 us (19%)
  other arithmetic  123 us (16%)
  blocking collectives  88.7 us (12%)
  local copies, waits for them, and re-layouts  25.1 us (3%)
  between operations  14.5 us (2%)
    dot_general x2, matrix products, per_device(): row_part = jnp.dot(expo_tab, col_scale, precision=lax.Precision.HIGHEST)  121 us
    dot_general x3, matrix products, per_device(): col_part = jnp.dot(row_weight, expo_tab, precision=lax.Precision.HIGHEST)  114 us
    psum x3, waiting for transfers between devices, per_device(): col_total = lax.psum(col_part, 'sec')  83.7 us
    reduce_scatter x1, waiting for transfers between devices, per_device(): lax.psum_scatter(lax.cond(is_student, lambda operand: lax.dot_general(ope...  59.9 us
    dot_general x1, matrix products, per_device(): logits = jnp.dot(unit_rows, prototypes, preferred_element_type=jnp.float32)  56.2 us
    convert_element_type x1, other arithmetic, per_device(): prob_gap = (weight[:, None] * (stud_probs - target)).astype(jnp.bfloat16)  53.1 us
    psum x2, blocking collectives, per_device(): row_total = lax.psum(row_part, 'proto')  43.2 us
    reduce_sum x1, other arithmetic, per_device(): jnp.sum(crop_exp, axis=1)  42.3 us
  transfers between devices with their start and end apart: 5, of which 4 were waited for; matrix products, arithmetic and copies ran while one was open for 7% of the time, Pallas kernels for 0%

commit v1 on v0

v1 whole, which is shorter than its diff:
```python
import functools
import math

import jax
import jax.numpy as jnp
from jax import lax
from jax.experimental import pallas as pl
from jax.experimental.pallas import tpu as pltpu
from jax.sharding import PartitionSpec as P

ITERS = 3
TEACH_TEMP = 0.07
STUD_TEMP = 0.1
LOG2E = math.log2(math.e)
LOW = -1e30
AXES = ("sec", "proto")
VMEM_LIMIT = 50 * 1024 * 1024


def unit_rows_of(features):
    values = features.astype(jnp.float32)
    scaled = values * lax.rsqrt(jnp.sum(values * values, axis=1, keepdims=True) + 1e-06)
    return scaled.astype(jnp.bfloat16)


def teacher_kernel(steps, sec_ref, rows_ref, proto_ref, expo_ref, top_ref, dots, top):
    step = pl.program_id(0)
    chunk = proto_ref.shape[1]

    @pl.when(step == 0)
    def _():
        top[...] = jnp.full_like(top, LOW)

    @pl.when(step < steps)
    def _():
        part = jnp.dot(rows_ref[...], proto_ref[...], preferred_element_type=jnp.float32)
        dots[step] = part
        top[...] = jnp.maximum(top[...], jnp.max(part, axis=1, keepdims=True))

    @pl.when(step >= steps)
    def _():
        shifted = dots[step - steps] - top[...]
        expo_ref[...] = jnp.exp2(shifted * (LOG2E / TEACH_TEMP)).astype(jnp.bfloat16)
        top_ref[...] = top[...]


def teacher_expo(sec_index, rows, prototypes, cols, chunk):
    count, width = rows.shape
    steps = cols // chunk
    return pl.pallas_call(
        functools.partial(teacher_kernel, steps),
        out_shape=(
            jax.ShapeDtypeStruct((count, cols), jnp.bfloat16),
            jax.ShapeDtypeStruct((count, 1), jnp.float32),
        ),
        grid_spec=pltpu.PrefetchScalarGridSpec(
            num_scalar_prefetch=1,
            grid=(2 * steps,),
            in_specs=[
                pl.BlockSpec((count, width), lambda s, sec: (0, 0)),
                pl.BlockSpec(
                    (width, chunk), lambda s, sec: (0, sec[0] * steps + jnp.minimum(s, steps - 1))
                ),
            ],
            out_specs=[
                pl.BlockSpec((count, chunk), lambda s, sec: (0, jnp.maximum(s - steps, 0))),
                pl.BlockSpec((count, 1), lambda s, sec: (0, 0)),
            ],
            scratch_shapes=[
                pltpu.VMEM((steps, count, chunk), jnp.float32),
                pltpu.VMEM((count, 1), jnp.float32),
            ],
        ),
        compiler_params=pltpu.CompilerParams(vmem_limit_bytes=VMEM_LIMIT),
        cost_estimate=pl.CostEstimate(
            flops=2 * count * width * cols, bytes_accessed=4 * width * cols, transcendentals=0
        ),
    )(sec_index, rows, prototypes)


def lanes_sum(block):
    total = block[:, 0:128]
    for at in range(128, block.shape[1], 128):
        total = total + block[:, at : at + 128]
    return total


def sweep_kernel(protos, factor_ref, weight_ref, expo_ref, total_ref, partial):
    step = pl.program_id(0)

    @pl.when(step == 0)
    def _():
        partial[...] = jnp.zeros_like(partial)

    expo = expo_ref[...].astype(jnp.float32) * factor_ref[...]
    col_total = jnp.sum(expo * weight_ref[...], axis=0, keepdims=True)
    col_scale = 1.0 / (protos * col_total)
    partial[...] += lanes_sum(expo * col_scale)
    total_ref[...] = jnp.sum(partial[...], axis=1, keepdims=True)


def sweep(factor, weight, expo_tab, protos, chunk):
    count, cols = expo_tab.shape
    return pl.pallas_call(
        functools.partial(sweep_kernel, protos),
        out_shape=jax.ShapeDtypeStruct((count, 1), jnp.float32),
        grid=(cols // chunk,),
        in_specs=[
            pl.BlockSpec((count, 1), lambda s: (0, 0)),
            pl.BlockSpec((count, 1), lambda s: (0, 0)),
            pl.BlockSpec((count, chunk), lambda s: (0, s)),
        ],
        out_specs=pl.BlockSpec((count, 1), lambda s: (0, 0)),
        scratch_shapes=[pltpu.VMEM((count, 128), jnp.float32)],
        compiler_params=pltpu.CompilerParams(vmem_limit_bytes=VMEM_LIMIT),
        cost_estimate=pl.CostEstimate(
            flops=6 * count * cols, bytes_accessed=2 * count * cols, transcendentals=0
        ),
    )(factor, weight, expo_tab)


def mean_kernel(protos, sec_ref, factor_ref, weight_ref, expo_ref, proto_ref, mean_ref, total_ref, partial):
    step = pl.program_id(0)

    @pl.when(step == 0)
    def _():
        partial[...] = jnp.zeros_like(partial)
        mean_ref[...] = jnp.zeros_like(mean_ref)

    expo = expo_ref[...].astype(jnp.float32) * factor_ref[...]
    col_total = jnp.sum(expo * weight_ref[...], axis=0, keepdims=True)
    col_scale = 1.0 / (protos * col_total)
    target = (expo * col_scale).astype(jnp.bfloat16)
    partial[...] += lanes_sum(target.astype(jnp.float32))
    total_ref[...] = jnp.sum(partial[...], axis=1, keepdims=True)
    mean_ref[...] += lax.dot_general(
        target, proto_ref[...], (((1,), (1,)), ((), ())), preferred_element_type=jnp.float32
    )


def target_mean(sec_index, factor, weight, expo_tab, prototypes, protos, chunk):
    count, cols = expo_tab.shape
    width = prototypes.shape[0]
    steps = cols // chunk
    return pl.pallas_call(
        functools.partial(mean_kernel, protos),
        out_shape=(
            jax.ShapeDtypeStruct((count, width), jnp.float32),
            jax.ShapeDtypeStruct((count, 1), jnp.float32),
        ),
        grid_spec=pltpu.PrefetchScalarGridSpec(
            num_scalar_prefetch=1,
            grid=(steps,),
            in_specs=[
                pl.BlockSpec((count, 1), lambda s, sec: (0, 0)),
                pl.BlockSpec((count, 1), lambda s, sec: (0, 0)),
                pl.BlockSpec((count, chunk), lambda s, sec: (0, s)),
                pl.BlockSpec((width, chunk), lambda s, sec: (0, sec[0] * steps + s)),
            ],
            out_specs=[
                pl.BlockSpec((count, width), lambda s, sec: (0, 0)),
                pl.BlockSpec((count, 1), lambda s, sec: (0, 0)),
            ],
            scratch_shapes=[pltpu.VMEM((count, 128), jnp.float32)],
        ),
        compiler_params=pltpu.CompilerParams(vmem_limit_bytes=VMEM_LIMIT),
        cost_estimate=pl.CostEstimate(
            flops=2 * count * width * cols, bytes_accessed=4 * width * cols, transcendentals=0
        ),
    )(sec_index, factor, weight, expo_tab, prototypes)


def student_kernel(sec_ref, rows_ref, now_ref, before_ref, grad_ref, top_ref, total_ref, dots, top, partial):
    step = pl.program_id(0)

    @pl.when(step == 0)
    def _():
        dots[1] = jnp.full(dots.shape[1:], LOW, jnp.float32)
        top[...] = jnp.full_like(top, 2 * LOW)
        partial[...] = jnp.zeros_like(partial)
        grad_ref[...] = jnp.zeros_like(grad_ref)

    slot = lax.rem(step, 2)
    dots[slot] = jnp.dot(rows_ref[...], now_ref[...], preferred_element_type=jnp.float32)
    before = dots[1 - slot]
    old_top = top[...]
    new_top = jnp.maximum(old_top, jnp.max(before, axis=1, keepdims=True))
    expo = jnp.exp2((before - new_top) * (LOG2E / STUD_TEMP))
    shrink = jnp.exp2((old_top - new_top) * (LOG2E / STUD_TEMP))
    top[...] = new_top
    partial[...] = partial[...] * shrink + lanes_sum(expo)
    grad_ref[...] = grad_ref[...] * shrink + lax.dot_general(
        expo.astype(jnp.bfloat16),
        before_ref[...],
        (((1,), (1,)), ((), ())),
        preferred_element_type=jnp.float32,
    )
    top_ref[...] = new_top
    total_ref[...] = jnp.sum(partial[...], axis=1, keepdims=True)


def student_mean(sec_index, rows, prototypes, cols, chunk):
    count, width = rows.shape
    steps = cols // chunk
    return pl.pallas_call(
        student_kernel,
        out_shape=(
            jax.ShapeDtypeStruct((count, width), jnp.float32),
            jax.ShapeDtypeStruct((count, 1), jnp.float32),
            jax.ShapeDtypeStruct((count, 1), jnp.float32),
        ),
        grid_spec=pltpu.PrefetchScalarGridSpec(
            num_scalar_prefetch=1,
            grid=(steps + 1,),
            in_specs=[
                pl.BlockSpec((count, width), lambda s, sec: (0, 0)),
                pl.BlockSpec(
                    (width, chunk), lambda s, sec: (0, sec[0] * steps + jnp.minimum(s, steps - 1))
                ),
                pl.BlockSpec(
                    (width, chunk), lambda s, sec: (0, sec[0] * steps + jnp.maximum(s - 1, 0))
                ),
            ],
            out_specs=[
                pl.BlockSpec((count, width), lambda s, sec: (0, 0)),
                pl.BlockSpec((count, 1), lambda s, sec: (0, 0)),
                pl.BlockSpec((count, 1), lambda s, sec: (0, 0)),
            ],
            scratch_shapes=[
                pltpu.VMEM((2, count, chunk), jnp.float32),
                pltpu.VMEM((count, 1), jnp.float32),
                pltpu.VMEM((count, 128), jnp.float32),
            ],
        ),
        compiler_params=pltpu.CompilerParams(vmem_limit_bytes=VMEM_LIMIT),
        cost_estimate=pl.CostEstimate(
            flops=4 * count * width * cols, bytes_accessed=4 * width * cols, transcendentals=0
        ),
    )(sec_index, rows, prototypes, prototypes)


def halve(blocks, axis):
    size = lax.axis_size(axis)
    index = lax.axis_index(axis)
    bit = 1
    while bit < size:
        rows, width = blocks.shape[1:]
        pairs = blocks.reshape(-1, 2, rows, width)
        mine = lax.rem(index // bit, 2)
        keep = lax.dynamic_index_in_dim(pairs, mine, 1, keepdims=False)
        give = lax.dynamic_index_in_dim(pairs, 1 - mine, 1, keepdims=False)
        got = lax.ppermute(
            give.astype(jnp.bfloat16), axis, [(i, i ^ bit) for i in range(size)]
        )
        blocks = keep + got.astype(jnp.float32)
        bit *= 2
    return blocks[0]


def per_device(features, prototypes, crop_sample, crop_live):
    row_count, width = features.shape
    proto_devs = lax.axis_size("proto")
    sec_devs = lax.axis_size("sec")
    teach_devs = sec_devs // 4
    first_dev = sec_devs // 2 - teach_devs // 2
    sample_count = row_count * teach_devs
    cols = prototypes.shape[1] // sec_devs
    protos = prototypes.shape[1] * proto_devs
    chunk = math.gcd(cols, 1024)
    sec_index = lax.axis_index("sec")
    sec_array = sec_index.astype(jnp.int32).reshape(1)
    is_student = jnp.logical_or(sec_index < first_dev, sec_index >= first_dev + teach_devs)

    own_rows = unit_rows_of(features)
    all_rows = lax.all_gather(own_rows, "sec", axis=0, tiled=True)
    teach_rows = all_rows[first_dev * row_count : first_dev * row_count + sample_count]
    expo_tab, local_top = teacher_expo(sec_array, teach_rows, prototypes, cols, chunk)
    row_top = lax.pmax(local_top, AXES)
    factor = jnp.exp2((local_top - row_top) * (LOG2E / TEACH_TEMP))
    weight = jnp.ones_like(factor)
    for _ in range(ITERS - 1):
        row_total = lax.psum(sweep(factor, weight, expo_tab, protos, chunk), AXES)
        weight = 1.0 / (sample_count * row_total)
    target_sums, target_total = target_mean(
        sec_array, factor, weight, expo_tab, prototypes, protos, chunk
    )
    target_sums, target_total = lax.psum((target_sums, target_total), AXES)
    targets_mean = target_sums / target_total

    parts, tops, totals = [], [], []
    for sec in range(sec_devs):
        if first_dev <= sec < first_dev + teach_devs:
            continue
        rows = all_rows[sec * row_count : (sec + 1) * row_count]
        part, top, total = student_mean(sec_array, rows, prototypes, cols, chunk)
        parts.append(part)
        tops.append(top)
        totals.append(total)
    tops = jnp.stack(tops)
    global_top = lax.pmax(tops, AXES)
    shrink = jnp.exp2((tops - global_top) * (LOG2E / STUD_TEMP))
    all_totals = lax.psum(jnp.stack(totals) * shrink, AXES)
    blank = jnp.zeros((teach_devs, row_count, width), jnp.float32)
    scaled = jnp.stack(parts) * shrink
    blocks = jnp.concatenate([scaled[:first_dev], blank, scaled[first_dev:]], axis=0)
    block = halve(blocks, "sec")
    stud_sums = halve(block.reshape(proto_devs, row_count // proto_devs, width), "proto")

    place = jnp.where(sec_index < first_dev, sec_index, sec_index - teach_devs)
    place = jnp.where(is_student, place, 0)
    own_top = lax.dynamic_index_in_dim(global_top, place, 0, keepdims=False)
    own_total = lax.dynamic_index_in_dim(all_totals, place, 0, keepdims=False)
    log_total = (own_top / STUD_TEMP + jnp.log(own_total))[:, 0]
    live = crop_live.astype(jnp.float32) * is_student.astype(jnp.float32)
    sample = jnp.where(is_student, crop_sample, 0)
    chosen = jnp.take(targets_mean, sample, axis=0)
    cross = jnp.sum(own_rows.astype(jnp.float32) * chosen, axis=1) / STUD_TEMP
    crop_loss = jnp.where(live > 0, live * (log_total - cross), 0.0)

    out_rows = row_count // proto_devs
    start = lax.axis_index("proto") * out_rows
    my_total = lax.dynamic_slice_in_dim(own_total, start, out_rows, 0)
    my_chosen = lax.dynamic_slice_in_dim(chosen, start, out_rows, 0)
    my_live = lax.dynamic_slice_in_dim(live, start, out_rows, 0)[:, None]
    gap = stud_sums / my_total - my_chosen
    embed_grad = jnp.where(my_live > 0, my_live * gap / STUD_TEMP, 0.0)
    return (crop_loss, embed_grad)


def solution(mesh):
    in_specs = (P("sec", None), P(None, "proto"), P("sec"), P("sec"))
    out_specs = (P("sec"), P(("sec", "proto"), None))
    return jax.shard_map(
        per_device, mesh=mesh, in_specs=in_specs, out_specs=out_specs, check_vma=False
    )
```

time: 760 us -> 450 us (0.59)
  matrix products: 358 us -> 0 us
  Pallas kernels: 0 us -> 112 us
  other arithmetic: 123 us -> 16 us
  blocking collectives: 88.7 us -> 175 us
  waiting for transfers between devices: 144 us -> 116 us
  local copies, waits for them, and re-layouts: 25.1 us -> 11.2 us
    dot_general x8 -> x0, matrix products: 358 us -> none  [the longest x2 121 us: per_device(): row_part = jnp.dot(expo_tab, col_scale, precision=lax.Precision.HIGHEST)]
    pallas_call x0 -> x7, Pallas kernels: none -> 112 us  [the longest x3 63.7 us: student_mean(): pl.pallas_call(student_kernel, out_shape=(jax.ShapeDtypeStruct((count, wi...]
    psum x3, blocking collectives: 64.8 us -> 130 us  [the longest x2 84.3 us: per_device(): row_total = lax.psum(sweep(factor, weight, expo_tab, protos, chunk), AXES)]
    reduce_scatter x1 -> x0, waiting for transfers between devices: 59.9 us -> none  [per_device(): lax.psum_scatter(lax.cond(is_student, lambda operand: lax.dot_general(ope...]
    convert_element_type x1, other arithmetic: 53.1 us -> 2.01 us  [unit_rows_of(): return scaled.astype(jnp.bfloat16)]
    reduce_sum x1, other arithmetic: 42.3 us -> 0.37 us  [per_device(): cross = jnp.sum(own_rows.astype(jnp.float32) * chosen, axis=1) / STUD_TEMP]
    all_gather x0 -> x1, waiting for transfers between devices: none -> 24.6 us  [per_device(): all_rows = lax.all_gather(own_rows, 'sec', axis=0, tiled=True)]
    another operation x1, local copies, waits for them, and re-layouts: 21 us -> 0.02 us
  transfers between devices with their start and end apart: 5 -> 7, of which waited for: 4 -> 5; matrix products, arithmetic and copies ran while one was open for 7% -> 2% of each run, Pallas kernels for 0% -> 7%
where the time goes in v1:
time: 450 us; the launch traced here: 448 us
  blocking collectives  175 us (39%)
  waiting for transfers between devices  116 us (26%)
  Pallas kernels  112 us (25%)
  other arithmetic  16 us (4%)
  between operations  14.4 us (3%)
  local copies, waits for them, and re-layouts  11.2 us (2%)
    psum x2, blocking collectives, per_device(): row_total = lax.psum(sweep(factor, weight, expo_tab, protos, chunk), AXES)  84.3 us
    psum x1, waiting for transfers between devices, per_device(): target_sums, target_total = lax.psum((target_sums, target_total), AXES)  78.4 us
    pallas_call x3, Pallas kernels, student_mean(): pl.pallas_call(student_kernel, out_shape=(jax.ShapeDtypeStruct((count, wi...  63.7 us
    psum x1, blocking collectives, per_device(): all_totals = lax.psum(jnp.stack(totals) * shrink, AXES)  46.2 us
    pmax x1, blocking collectives, per_device(): global_top = lax.pmax(tops, AXES)  44.8 us
    all_gather x1, waiting for transfers between devices, per_device(): all_rows = lax.all_gather(own_rows, 'sec', axis=0, tiled=True)  24.6 us
    pallas_call x2, Pallas kernels, sweep(): pl.pallas_call(functools.partial(sweep_kernel, protos), out_shape=jax.Sha...  18.1 us
    pallas_call x1, Pallas kernels, teacher_expo(): pl.pallas_call(functools.partial(teacher_kernel, steps), out_shape=(jax.S...  15.1 us
  transfers between devices with their start and end apart: 7, of which 5 were waited for; matrix products, arithmetic and copies ran while one was open for 2% of the time, Pallas kernels for 7%

profile of v1, /device:TPU:0, one launch (start us, length us, event | category | flops | bytes accessed | tf_op | source)
XLA Modules:
  0.0 448.5 jit_solution(421503364276104824)
XLA Ops:
  8.4 2.0 fusion.1
  11.3 24.6 %all-gather.2.cloned.1.call-done = bf16[2048,512]{1,0:T(8,128)(2,1)} async-done(((bf16[512,512]{1,0:T(8,128)(2,1)}), bf16[2048,512]{1,0:T(8,128)(2,1)}) %all-gather.2.cloned.1.call-update) | async-done | bytes 2097168 | tf_op jit(solution)/shard_map/all_gather | solution.py:275
  35.9 1.7 fusion.13
  37.6 21.2 %shard_map.61 = (f32[512,512]{1,0:T(8,128)S(1)}, f32[512,1]{1,0:T(8,128)S(1)}, f32[512,1]{1,0:T(8,128)S(1)}) custom-call(s32[1]{0:T(128)} %bitcast.sec_ref, bf16[512,512]{1,0:T(8,128)(2,1)S(1)} %get-tuple-element.43.rows_ref, bf16[512,32768]{1,0:T(8,128)(2,1)} %proto_ref.3, bf16[512,32768]{1,0:T(8,128)(2,1)} %proto_ref.3), custom_call_target="tpu_custom_call" | custom-call | flops 8589934592 | bytes 16777216 | tf_op jit(solution)/shard_map/pallas_call | solution.py:205
  60.2 21.3 %shard_map.60 = (f32[512,512]{1,0:T(8,128)S(1)}, f32[512,1]{1,0:T(8,128)S(1)}, f32[512,1]{1,0:T(8,128)S(1)}) custom-call(s32[1]{0:T(128)} %bitcast.sec_ref, bf16[512,512]{1,0:T(8,128)(2,1)S(1)} %get-tuple-element.44.rows_ref, bf16[512,32768]{1,0:T(8,128)(2,1)} %proto_ref.3, bf16[512,32768]{1,0:T(8,128)(2,1)} %proto_ref.3), custom_call_target="tpu_custom_call" | custom-call | flops 8589934592 | bytes 16777216 | tf_op jit(solution)/shard_map/pallas_call | solution.py:205
  83.5 21.3 %shard_map.59 = (f32[512,512]{1,0:T(8,128)S(1)}, f32[512,1]{1,0:T(8,128)S(1)}, f32[512,1]{1,0:T(8,128)S(1)}) custom-call(s32[1]{0:T(128)} %bitcast.sec_ref, bf16[512,512]{1,0:T(8,128)(2,1)S(1)} %get-tuple-element.45.rows_ref, bf16[512,32768]{1,0:T(8,128)(2,1)} %proto_ref.3, bf16[512,32768]{1,0:T(8,128)(2,1)} %proto_ref.3), custom_call_target="tpu_custom_call" | custom-call | flops 8589934592 | bytes 16777216 | tf_op jit(solution)/shard_map/pallas_call | solution.py:205
  106.7 15.1 %shard_map.62 = (bf16[512,8192]{1,0:T(8,128)(2,1)}, f32[512,1]{1,0:T(8,128)S(1)}) custom-call(s32[1]{0:T(128)} %bitcast.sec_ref, bf16[512,512]{1,0:T(8,128)(2,1)S(1)} %get-tuple-element.42.rows_ref, bf16[512,32768]{1,0:T(8,128)(2,1)} %proto_ref.3), custom_call_target="tpu_custom_call" | custom-call | flops 4294967296 | bytes 16777216 | tf_op jit(solution)/shard_map/pallas_call | solution.py:50
  123.2 44.8 %all-reduce.1 = (f32[3,512,1]{1,2,0:T(1,128)S(1)}, f32[512,1]{1,0:T(8,128)S(1)}) all-reduce(f32[3,512,1]{1,2,0:T(1,128)S(1)} %pad_maximum_fusion.1, f32[512,1]{1,0:T(8,128)S(1)} %get-tuple-element.21), channel_id=1, replica_groups=mesh['sec'=4,'proto'=8] {'sec','proto'}, use_global_device_ids=true, to_apply=%region_1.0 | all-reduce | flops 2048 | bytes 16384 | tf_op jit(solution)/shard_map/pmax | solution.py:300
  168.0 1.5 maximum_multiply_fusion
  170.8 1.7 copy-done.7
  172.5 9.0 %shard_map.63 = f32[512,1]{1,0:T(8,128)S(1)} custom-call(f32[512,1]{1,0:T(8,128)S(1)} %multiply_exponential_fusion.factor_ref, f32[512,1]{1,0:T(8,128)S(1)} %broadcast_3_weight_ref.2.weight_ref, bf16[512,8192]{1,0:T(8,128)(2,1)} %get-tuple-element.22.expo_ref), custom_call_target="tpu_custom_call" | custom-call | flops 25165824 | bytes 8388608 | tf_op jit(solution)/shard_map/pallas_call | solution.py:104
  181.5 41.7 %psum.36 = f32[512,1]{1,0:T(8,128)S(1)} all-reduce(f32[512,1]{1,0:T(8,128)S(1)} %shard_map.63), channel_id=1, replica_groups=mesh['sec'=4,'proto'=8] {'sec','proto'}, use_global_device_ids=true, to_apply=%region_4.0 | all-reduce | flops 512 | bytes 4096 | tf_op jit(solution)/shard_map/psum | solution.py:282
  223.2 9.0 %shard_map.64 = f32[512,1]{1,0:T(8,128)S(1)} custom-call(f32[512,1]{1,0:T(8,128)S(1)} %multiply_exponential_fusion.factor_ref, f32[512,1]{1,0:T(8,128)S(1)} %multiply_divide_fusion.1.weight_ref, bf16[512,8192]{1,0:T(8,128)(2,1)} %get-tuple-element.22.expo_ref), custom_call_target="tpu_custom_call" | custom-call | flops 25165824 | bytes 8388608 | tf_op jit(solution)/shard_map/pallas_call | solution.py:104
  232.3 42.6 %psum.37 = f32[512,1]{1,0:T(8,128)S(1)} all-reduce(f32[512,1]{1,0:T(8,128)S(1)} %shard_map.64), channel_id=1, replica_groups=mesh['sec'=4,'proto'=8] {'sec','proto'}, use_global_device_ids=true, to_apply=%region_5.0 | all-reduce | flops 512 | bytes 4096 | tf_op jit(solution)/shard_map/psum | solution.py:282
  274.9 14.6 %shard_map.65 = (f32[512,512]{1,0:T(8,128)}, f32[512,1]{1,0:T(8,128)S(1)}) custom-call(s32[1]{0:T(128)} %bitcast.sec_ref, f32[512,1]{1,0:T(8,128)S(1)} %multiply_exponential_fusion.factor_ref, f32[512,1]{1,0:T(8,128)S(1)} %multiply_divide_fusion.weight_ref, bf16[512,8192]{1,0:T(8,128)(2,1)} %get-tuple-element.22.expo_ref, bf16[512,32768]{1,0:T(8,128)(2,1)} %proto_ref.3), custom_call_target="tpu_custom_call" | custom-call | flops 4294967296 | bytes 16777216 | tf_op jit(solution)/shard_map/pallas_call | solution.py:145
  289.6 2.3 bitcast_add_fusion
  293.5 46.2 %all-reduce = (f32[3,512,1]{1,2,0:T(1,128)S(1)}, f32[512]{0:T(512)S(1)}) all-reduce(f32[3,512,1]{1,2,0:T(1,128)S(1)} %get-tuple-element.40, f32[512]{0:T(512)S(1)} %reduce.6), channel_id=1, replica_groups=mesh['sec'=4,'proto'=8] {'sec','proto'}, use_global_device_ids=true, to_apply=%region_2.0 | all-reduce | flops 2048 | bytes 16384 | tf_op jit(solution)/shard_map/psum | solution.py:302
  339.7 78.4 %all-reduce.4.cloned.1.call-done = f32[512,512]{1,0:T(8,128)} async-done(((f32[512,512]{1,0:T(8,128)}), f32[512,512]{1,0:T(8,128)}) %all-reduce.4.cloned.1.call-update) | async-done | bytes 1048592 | tf_op jit(solution)/shard_map/psum | solution.py:287
  418.1 1.4 broadcast_divide_fusion
  419.5 2.3 gather_fusion
  423.2 1.5 collective-permute-start.2
  425.1 5.4 %collective-permute-done.2 = bf16[4,64,512]{2,1,0:T(8,128)(2,1)S(1)} collective-permute-done((bf16[4,64,512]{2,1,0:T(8,128)(2,1)S(1)}, bf16[4,64,512]{2,1,0:T(8,128)(2,1)S(1)}, u32[]{:S(2)}, u32[]{:S(2)}) %collective-permute-start.2) | collective-permute-done | bytes 262176 | tf_op jit(solution)/shard_map/ppermute | solution.py:252
  431.8 3.8 collective-permute-done.3
  436.7 4.2 collective-permute-done.4
  (67 shorter events, 16.6 us)
Async XLA Ops:
  7.2 28.8 %all-gather.2.cloned.1.call-start = ((), (), s32[]{:S(2)}) async-start(), calls=%async_computation | async-start | bytes 2621440 | tf_op jit(solution)/shard_map/all_gather | solution.py:275
  10.5 407.6 %all-reduce.4.cloned.1.call-start = ((), (), s32[]{:S(2)}) async-start(), calls=%async_computation.1 | async-start | bytes 2097152 | tf_op jit(solution)/shard_map/psum | solution.py:287
  58.8 0.7 copy-start.1
  59.5 0.7 copy-start.6
  81.5 0.7 copy-start.3
  104.8 1.1 copy-start
  105.8 0.7 copy-start.5
  106.7 15.1 %copy-start.2 = (f32[512,1]{1,0:T(8,128)S(1)}, f32[512,1]{1,0:T(8,128)}, u32[]{:S(2)}) copy-start(f32[512,1]{1,0:T(8,128)} %copy-done.1) | copy-start | bytes 6148
  106.7 15.3 %copy-start.4 = (f32[512,1]{1,0:T(8,128)S(1)}, f32[512,1]{1,0:T(8,128)}, u32[]{:S(2)}) copy-start(f32[512,1]{1,0:T(8,128)} %copy-done.3) | copy-start | bytes 6148
  170.5 2.0 copy-start.7
  170.6 119.0 %collective-permute-start = (bf16[2,512,512]{2,1,0:T(8,128)(2,1)S(1)}, bf16[2,512,512]{2,1,0:T(8,128)(2,1)}, u32[]{:S(2)}, u32[]{:S(2)}) collective-permute-start(bf16[2,512,512]{2,1,0:T(8,128)(2,1)S(1)} %fusion.2), channel_id=1, source_target_pairs={{0,8},{8,0},{16,24},{24,16},{1,9},{9,1},{17,25},{25,17},{2,10},{10... | collective-permute-start | bytes 3145736 | tf_op jit(solution)/shard_map/ppermute | solution.py:252
  292.8 129.0 %collective-permute-start.1 = (bf16[1,512,512]{2,1,0:T(8,128)(2,1)}, bf16[1,512,512]{2,1,0:T(8,128)(2,1)}, u32[]{:S(2)}, u32[]{:S(2)}) collective-permute-start(bf16[1,512,512]{2,1,0:T(8,128)(2,1)} %dynamic-slice_convert_fusion), channel_id=1, source_target_pairs={{0,16},{8,24},{16,0},{24,8},{1,17},{9,25},{17,1},{25,9},{2,18},{10... | collective-permute-start | bytes 1572872 | tf_op jit(solution)/shard_map/ppermute | solution.py:252
  421.8 2.9 copy-start.8
  421.8 2.9 copy-start.9
  421.8 9.4 %copy-start.10 = (s32[512]{0:T(512)S(1)}, s32[512]{0:T(512)}, u32[]{:S(2)}) copy-start(s32[512]{0:T(512)} %param.7) | copy-start | bytes 6148
  423.2 7.3 %collective-permute-start.2 = (bf16[4,64,512]{2,1,0:T(8,128)(2,1)S(1)}, bf16[4,64,512]{2,1,0:T(8,128)(2,1)S(1)}, u32[]{:S(2)}, u32[]{:S(2)}) collective-permute-start(bf16[4,64,512]{2,1,0:T(8,128)(2,1)S(1)} %fusion.3), channel_id=1, source_target_pairs={{0,1},{1,0},{2,3},{3,2},{4,5},{5,4},{6,7},{7,6},{8,9},{9,8},{10,11... | collective-permute-start | bytes 786440 | tf_op jit(solution)/shard_map/ppermute | solution.py:252
  430.6 5.0 %collective-permute-start.3 = (bf16[2,64,512]{2,1,0:T(8,128)(2,1)S(1)}, bf16[2,64,512]{2,1,0:T(8,128)(2,1)S(1)}, u32[]{:S(2)}, u32[]{:S(2)}) collective-permute-start(bf16[2,64,512]{2,1,0:T(8,128)(2,1)S(1)} %fusion.4), channel_id=1, source_target_pairs={{0,2},{1,3},{2,0},{3,1},{4,6},{5,7},{6,4},{7,5},{8,10},{9,11},{10,... | collective-permute-start | bytes 393224 | tf_op jit(solution)/shard_map/ppermute | solution.py:252
  435.7 5.2 %collective-permute-start.4 = (bf16[1,64,512]{2,1,0:T(8,128)(2,1)S(1)}, bf16[1,64,512]{2,1,0:T(8,128)(2,1)S(1)}, u32[]{:S(2)}, u32[]{:S(2)}) collective-permute-start(bf16[1,64,512]{2,1,0:T(8,128)(2,1)S(1)} %dynamic-slice_convert_fusion.2), channel_id=1, source_target_pairs={{0,4},{1,5},{2,6},{3,7},{4,0},{5,1},{6,2},{7,3},{8,12},{9,13},{10,... | collective-permute-start | bytes 196616 | tf_op jit(solution)/shard_map/ppermute | solution.py:252
Sparse Core Ops, SparseCore 0:
  10.6 25.2 all-gather.1
  289.7 128.3 all-reduce.3

commit v2 on v1

v2 whole, which is shorter than its diff:
```python
import functools
import math

import jax
import jax.numpy as jnp
from jax import lax
from jax.experimental import pallas as pl
from jax.experimental.pallas import tpu as pltpu
from jax.sharding import PartitionSpec as P

ITERS = 3
TEACH_TEMP = 0.07
STUD_TEMP = 0.1
LOG2E = math.log2(math.e)
LOW = -1e30
AXES = ("sec", "proto")
VMEM_LIMIT = 50 * 1024 * 1024


def unit_rows_of(features):
    values = features.astype(jnp.float32)
    scaled = values * lax.rsqrt(jnp.sum(values * values, axis=1, keepdims=True) + 1e-06)
    return scaled.astype(jnp.bfloat16)


def teacher_kernel(rows_ref_sec, rows_ref, proto_ref, expo_ref, top_ref):
    count = rows_ref.shape[0]
    half = count // 2
    parts = [
        jnp.dot(rows_ref[at : at + half], proto_ref[...], preferred_element_type=jnp.float32)
        for at in (0, half)
    ]
    for at, part in zip((0, half), parts):
        top = jnp.max(part, axis=1, keepdims=True)
        top_ref[0, at : at + half] = top
        expo_ref[at : at + half] = jnp.exp2((part - top) * (LOG2E / TEACH_TEMP)).astype(
            jnp.bfloat16
        )


def teacher_expo(sec_index, rows, prototypes, cols, chunk):
    count, width = rows.shape
    steps = cols // chunk
    return pl.pallas_call(
        teacher_kernel,
        out_shape=(
            jax.ShapeDtypeStruct((count, cols), jnp.bfloat16),
            jax.ShapeDtypeStruct((steps, count, 1), jnp.float32),
        ),
        grid_spec=pltpu.PrefetchScalarGridSpec(
            num_scalar_prefetch=1,
            grid=(steps,),
            in_specs=[
                pl.BlockSpec((count, width), lambda s, sec: (0, 0)),
                pl.BlockSpec((width, chunk), lambda s, sec: (0, sec[0] * steps + s)),
            ],
            out_specs=[
                pl.BlockSpec((count, chunk), lambda s, sec: (0, s)),
                pl.BlockSpec((1, count, 1), lambda s, sec: (s, 0, 0)),
            ],
        ),
        compiler_params=pltpu.CompilerParams(vmem_limit_bytes=VMEM_LIMIT),
        cost_estimate=pl.CostEstimate(
            flops=2 * count * width * cols, bytes_accessed=4 * width * cols, transcendentals=0
        ),
    )(sec_index, rows, prototypes)


def lanes_sum(block):
    total = block[:, 0:128]
    for at in range(128, block.shape[1], 128):
        total = total + block[:, at : at + 128]
    return total


def sweep_kernel(protos, factor_ref, weight_ref, expo_ref, total_ref, partial):
    step = pl.program_id(0)

    @pl.when(step == 0)
    def _():
        partial[...] = jnp.zeros_like(partial)

    expo = expo_ref[...].astype(jnp.float32) * factor_ref[0]
    col_total = jnp.sum(expo * weight_ref[...], axis=0, keepdims=True)
    col_scale = 1.0 / (protos * col_total)
    partial[...] += lanes_sum(expo * col_scale)
    total_ref[...] = jnp.sum(partial[...], axis=1, keepdims=True)


def sweep(factor, weight, expo_tab, protos, chunk):
    count, cols = expo_tab.shape
    return pl.pallas_call(
        functools.partial(sweep_kernel, protos),
        out_shape=jax.ShapeDtypeStruct((count, 1), jnp.float32),
        grid=(cols // chunk,),
        in_specs=[
            pl.BlockSpec((1, count, 1), lambda s: (s, 0, 0)),
            pl.BlockSpec((count, 1), lambda s: (0, 0)),
            pl.BlockSpec((count, chunk), lambda s: (0, s)),
        ],
        out_specs=pl.BlockSpec((count, 1), lambda s: (0, 0)),
        scratch_shapes=[pltpu.VMEM((count, 128), jnp.float32)],
        compiler_params=pltpu.CompilerParams(vmem_limit_bytes=VMEM_LIMIT),
        cost_estimate=pl.CostEstimate(
            flops=6 * count * cols, bytes_accessed=2 * count * cols, transcendentals=0
        ),
    )(factor, weight, expo_tab)


def mean_kernel(protos, sec_ref, factor_ref, weight_ref, expo_ref, proto_ref, mean_ref, total_ref, partial):
    step = pl.program_id(0)

    @pl.when(step == 0)
    def _():
        partial[...] = jnp.zeros_like(partial)
        mean_ref[...] = jnp.zeros_like(mean_ref)

    expo = expo_ref[...].astype(jnp.float32) * factor_ref[0]
    col_total = jnp.sum(expo * weight_ref[...], axis=0, keepdims=True)
    col_scale = 1.0 / (protos * col_total)
    target = (expo * col_scale).astype(jnp.bfloat16)
    partial[...] += lanes_sum(target.astype(jnp.float32))
    total_ref[...] = jnp.sum(partial[...], axis=1, keepdims=True)
    mean_ref[...] += lax.dot_general(
        target, proto_ref[...], (((1,), (1,)), ((), ())), preferred_element_type=jnp.float32
    )


def target_mean(sec_index, factor, weight, expo_tab, prototypes, protos, chunk):
    count, cols = expo_tab.shape
    width = prototypes.shape[0]
    steps = cols // chunk
    return pl.pallas_call(
        functools.partial(mean_kernel, protos),
        out_shape=(
            jax.ShapeDtypeStruct((count, width), jnp.float32),
            jax.ShapeDtypeStruct((count, 1), jnp.float32),
        ),
        grid_spec=pltpu.PrefetchScalarGridSpec(
            num_scalar_prefetch=1,
            grid=(steps,),
            in_specs=[
                pl.BlockSpec((1, count, 1), lambda s, sec: (s, 0, 0)),
                pl.BlockSpec((count, 1), lambda s, sec: (0, 0)),
                pl.BlockSpec((count, chunk), lambda s, sec: (0, s)),
                pl.BlockSpec((width, chunk), lambda s, sec: (0, sec[0] * steps + s)),
            ],
            out_specs=[
                pl.BlockSpec((count, width), lambda s, sec: (0, 0)),
                pl.BlockSpec((count, 1), lambda s, sec: (0, 0)),
            ],
            scratch_shapes=[pltpu.VMEM((count, 128), jnp.float32)],
        ),
        compiler_params=pltpu.CompilerParams(vmem_limit_bytes=VMEM_LIMIT),
        cost_estimate=pl.CostEstimate(
            flops=2 * count * width * cols, bytes_accessed=4 * width * cols, transcendentals=0
        ),
    )(sec_index, factor, weight, expo_tab, prototypes)


def student_kernel(block, sec_ref, rows_ref, proto_ref, grad_ref, top_ref, total_ref, partial):
    step = pl.program_id(0)

    @pl.when(step == 0)
    def _():
        top_ref[...] = jnp.full_like(top_ref, LOW)
        partial[...] = jnp.zeros_like(partial)
        grad_ref[...] = jnp.zeros_like(grad_ref)

    def dots_of(at):
        return jnp.dot(
            rows_ref[at : at + block], proto_ref[...], preferred_element_type=jnp.float32
        )

    starts = list(range(0, rows_ref.shape[0], block))
    ahead = dots_of(starts[0])
    for turn, at in enumerate(starts):
        dots = ahead
        if turn + 1 < len(starts):
            ahead = dots_of(starts[turn + 1])
        old_top = top_ref[at : at + block]
        new_top = jnp.maximum(old_top, jnp.max(dots, axis=1, keepdims=True))
        expo = jnp.exp2((dots - new_top) * (LOG2E / STUD_TEMP))
        shrink = jnp.exp2((old_top - new_top) * (LOG2E / STUD_TEMP))
        top_ref[at : at + block] = new_top
        partial[at : at + block] = partial[at : at + block] * shrink + lanes_sum(expo)
        grad_ref[at : at + block] = grad_ref[at : at + block] * shrink + lax.dot_general(
            expo.astype(jnp.bfloat16),
            proto_ref[...],
            (((1,), (1,)), ((), ())),
            preferred_element_type=jnp.float32,
        )

    @pl.when(step == pl.num_programs(0) - 1)
    def _():
        total_ref[...] = jnp.sum(partial[...], axis=1, keepdims=True)


def student_mean(sec_index, rows, prototypes, cols, chunk, block):
    count, width = rows.shape
    steps = cols // chunk
    return pl.pallas_call(
        functools.partial(student_kernel, block),
        out_shape=(
            jax.ShapeDtypeStruct((count, width), jnp.float32),
            jax.ShapeDtypeStruct((count, 1), jnp.float32),
            jax.ShapeDtypeStruct((count, 1), jnp.float32),
        ),
        grid_spec=pltpu.PrefetchScalarGridSpec(
            num_scalar_prefetch=1,
            grid=(steps,),
            in_specs=[
                pl.BlockSpec((count, width), lambda s, sec: (0, 0)),
                pl.BlockSpec((width, chunk), lambda s, sec: (0, sec[0] * steps + s)),
            ],
            out_specs=[
                pl.BlockSpec((count, width), lambda s, sec: (0, 0)),
                pl.BlockSpec((count, 1), lambda s, sec: (0, 0)),
                pl.BlockSpec((count, 1), lambda s, sec: (0, 0)),
            ],
            scratch_shapes=[pltpu.VMEM((count, 128), jnp.float32)],
        ),
        compiler_params=pltpu.CompilerParams(vmem_limit_bytes=VMEM_LIMIT),
        cost_estimate=pl.CostEstimate(
            flops=4 * count * width * cols, bytes_accessed=4 * width * cols, transcendentals=0
        ),
    )(sec_index, rows, prototypes)


def share_kernel(combine, sizes, value_ref, out_ref, *scratch):
    slots = scratch[: len(AXES)]
    send_sems, recv_sems = scratch[len(AXES) :]
    barrier = pltpu.get_barrier_semaphore()
    peers = 0
    for axis, size in zip(AXES, sizes):
        me = lax.axis_index(axis)
        for shift in range(1, size):
            pl.semaphore_signal(
                barrier,
                inc=1,
                device_id={axis: lax.rem(me + shift, size)},
                device_id_type=pl.DeviceIdType.MESH,
            )
            peers += 1
    pl.semaphore_wait(barrier, peers)
    current = value_ref[...]
    number = 0
    for axis, size, slot in zip(AXES, sizes, slots):
        me = lax.axis_index(axis)
        slot[me] = current
        copies = []
        for shift in range(1, size):
            copy = pltpu.make_async_remote_copy(
                src_ref=slot.at[me],
                dst_ref=slot.at[me],
                send_sem=send_sems.at[number],
                recv_sem=recv_sems.at[number],
                device_id={axis: lax.rem(me + shift, size)},
                device_id_type=pl.DeviceIdType.MESH,
            )
            copy.start()
            copies.append(copy)
            number += 1
        for copy in copies:
            copy.wait()
        current = slot[0]
        for other in range(1, size):
            current = combine(current, slot[other])
    out_ref[...] = current


def share(combine, vectors, collective_id):
    sizes = tuple(lax.axis_size(axis) for axis in AXES)
    flat = jnp.concatenate([vector.reshape(-1) for vector in vectors])
    count = flat.shape[0]
    rows = -(-count // 1024) * 8
    flat = jnp.pad(flat, (0, rows * 128 - count)).reshape(rows, 128)
    peers = sum(sizes) - len(sizes)
    shared = pl.pallas_call(
        functools.partial(share_kernel, combine, sizes),
        out_shape=jax.ShapeDtypeStruct((rows, 128), jnp.float32),
        in_specs=[pl.BlockSpec(memory_space=pltpu.VMEM)],
        out_specs=pl.BlockSpec(memory_space=pltpu.VMEM),
        scratch_shapes=[pltpu.VMEM((size, rows, 128), jnp.float32) for size in sizes]
        + [pltpu.SemaphoreType.DMA((peers,)), pltpu.SemaphoreType.DMA((peers,))],
        compiler_params=pltpu.CompilerParams(collective_id=collective_id, has_side_effects=True),
    )(flat).reshape(-1)
    results, at = [], 0
    for vector in vectors:
        results.append(shared[at : at + vector.size].reshape(vector.shape))
        at += vector.size
    return results


def halve(blocks, axis):
    size = lax.axis_size(axis)
    index = lax.axis_index(axis)
    bit = 1
    while bit < size:
        rows, width = blocks.shape[1:]
        pairs = blocks.reshape(-1, 2, rows, width)
        mine = lax.rem(index // bit, 2)
        keep = lax.dynamic_index_in_dim(pairs, mine, 1, keepdims=False)
        give = lax.dynamic_index_in_dim(pairs, 1 - mine, 1, keepdims=False)
        got = lax.ppermute(
            give.astype(jnp.bfloat16), axis, [(i, i ^ bit) for i in range(size)]
        )
        blocks = keep + got.astype(jnp.float32)
        bit *= 2
    return blocks[0]


def per_device(features, prototypes, crop_sample, crop_live):
    row_count, width = features.shape
    proto_devs = lax.axis_size("proto")
    sec_devs = lax.axis_size("sec")
    teach_devs = sec_devs // 4
    first_dev = sec_devs // 2 - teach_devs // 2
    sample_count = row_count * teach_devs
    cols = prototypes.shape[1] // sec_devs
    protos = prototypes.shape[1] * proto_devs
    chunk = math.gcd(cols, 2048)
    sec_index = lax.axis_index("sec")
    sec_array = sec_index.astype(jnp.int32).reshape(1)
    is_student = jnp.logical_or(sec_index < first_dev, sec_index >= first_dev + teach_devs)

    own_rows = unit_rows_of(features)
    sample = jnp.where(is_student, crop_sample, 0)
    digits = jnp.concatenate([sample // 128, sample % 128]).astype(jnp.bfloat16)
    extra = -(-digits.shape[0] // (16 * width)) * 16
    digits = jnp.pad(digits, (0, extra * width - digits.shape[0])).reshape(extra, width)
    packed = lax.all_gather(jnp.concatenate([own_rows, digits]), "sec", axis=0)
    all_rows = packed[:, :row_count]
    all_digits = packed[:, row_count:].reshape(sec_devs, -1)[:, : 2 * row_count].astype(jnp.int32)
    all_samples = all_digits[:, :row_count] * 128 + all_digits[:, row_count:]

    def students_of(blocks):
        return jnp.concatenate([blocks[:first_dev], blocks[first_dev + teach_devs :]])

    stud_rows = students_of(all_rows).reshape(-1, width)
    stud_samples = students_of(all_samples).reshape(-1)
    teach_rows = all_rows[first_dev : first_dev + teach_devs].reshape(-1, width)

    stud_part, stud_top, stud_total = student_mean(
        sec_array, stud_rows, prototypes, cols, chunk, row_count
    )
    expo_tab, chunk_tops = teacher_expo(sec_array, teach_rows, prototypes, cols, chunk)
    row_top, global_top = share(jnp.maximum, [jnp.max(chunk_tops, axis=0), stud_top], 0)
    factor = jnp.exp2((chunk_tops - row_top) * (LOG2E / TEACH_TEMP))
    weight = jnp.ones_like(row_top)
    for turn in range(ITERS - 1):
        row_part = sweep(factor, weight, expo_tab, protos, chunk)
        (row_total,) = share(jnp.add, [row_part], 1 + turn)
        weight = 1.0 / (sample_count * row_total)
    target_part, target_total = target_mean(
        sec_array, factor, weight, expo_tab, prototypes, protos, chunk
    )
    pick = (stud_samples[:, None] == jnp.arange(sample_count)[None, :]).astype(jnp.bfloat16)
    chosen_part = jnp.dot(
        pick, target_part.astype(jnp.bfloat16), preferred_element_type=jnp.float32
    )
    cross_part = jnp.sum(stud_rows.astype(jnp.float32) * chosen_part, axis=1, keepdims=True)
    shrink = jnp.exp2((stud_top - global_top) * (LOG2E / STUD_TEMP))
    target_total, stud_total, cross = share(
        jnp.add, [target_total, stud_total * shrink, cross_part], ITERS
    )
    chosen_total = jnp.take(target_total[:, 0], stud_samples)[:, None]
    gap_part = stud_part * (shrink / stud_total) - chosen_part / chosen_total
    gap_part = gap_part.reshape(-1, row_count, width)
    blank = jnp.zeros((teach_devs, row_count, width), jnp.float32)
    blocks = jnp.concatenate([gap_part[:first_dev], blank, gap_part[first_dev:]])
    block = halve(blocks, "sec")
    gap = halve(block.reshape(proto_devs, row_count // proto_devs, width), "proto")

    loss = global_top / STUD_TEMP + jnp.log(stud_total) - cross / chosen_total / STUD_TEMP
    place = jnp.where(sec_index < first_dev, sec_index, sec_index - teach_devs)
    place = jnp.where(is_student, place, 0)
    own_loss = lax.dynamic_index_in_dim(loss.reshape(-1, row_count), place, 0, keepdims=False)
    live = crop_live.astype(jnp.float32) * is_student.astype(jnp.float32)
    crop_loss = jnp.where(live > 0, live * own_loss, 0.0)
    out_rows = row_count // proto_devs
    start = lax.axis_index("proto") * out_rows
    my_live = lax.dynamic_slice_in_dim(live, start, out_rows, 0)[:, None]
    embed_grad = jnp.where(my_live > 0, my_live * gap / STUD_TEMP, 0.0)
    return (crop_loss, embed_grad)


def solution(mesh):
    in_specs = (P("sec", None), P(None, "proto"), P("sec"), P("sec"))
    out_specs = (P("sec"), P(("sec", "proto"), None))
    return jax.shard_map(
        per_device, mesh=mesh, in_specs=in_specs, out_specs=out_specs, check_vma=False
    )
```

time: 450 us -> 244 us (0.54)
  blocking collectives: 175 us -> 0 us
  waiting for transfers between devices: 116 us -> 53.4 us
  local copies, waits for them, and re-layouts: 11.2 us -> 28 us
  other arithmetic: 16 us -> 23.6 us
    psum x3 -> x0, blocking collectives: 130 us -> none  [the longest x2 84.3 us: per_device(): row_total = lax.psum(sweep(factor, weight, expo_tab, protos, chunk), AXES)]
    psum x1 -> x0, waiting for transfers between devices: 78.4 us -> none  [per_device(): target_sums, target_total = lax.psum((target_sums, target_total), AXES)]
    pmax x1 -> x0, blocking collectives: 44.8 us -> none  [per_device(): global_top = lax.pmax(tops, AXES)]
    ppermute x5, waiting for transfers between devices: 13.4 us -> 28.1 us  [halve(): lax.ppermute(give.astype(jnp.bfloat16), axis, [(i, i ^ bit) for i in rang...]
    pallas_call x4 -> x6, Pallas kernels: 78.9 us -> 88 us  [the longest x4 44 us: share(): pl.pallas_call(functools.partial(share_kernel, combine, sizes), out_shape...]
    gather x1 -> x2, local copies, waits for them, and re-layouts: 2.34 us -> 9.49 us  [per_device(): chosen_total = jnp.take(target_total[:, 0], stud_samples)[:, None]]
    unnamed x23 -> x36, local copies, waits for them, and re-layouts: 5.58 us -> 10.9 us
  transfers between devices with their start and end apart: 7 -> 6, of which waited for: 5 -> 6; matrix products, arithmetic and copies ran while one was open for 2% -> 0% of each run, Pallas kernels for 7% -> 0%
where the time goes in v2:
time: 244 us; the launch traced here: 243 us
  Pallas kernels  115 us (47%)
  waiting for transfers between devices  53.4 us (22%)
  local copies, waits for them, and re-layouts  28 us (11%)
  other arithmetic  23.6 us (10%)
  between operations  14.5 us (6%)
  starting transfers between devices  5.94 us (2%)
  matrix products  2.75 us (1%)
    pallas_call x4, Pallas kernels, share(): pl.pallas_call(functools.partial(share_kernel, combine, sizes), out_shape...  44 us
    pallas_call x1, Pallas kernels, student_mean(): pl.pallas_call(functools.partial(student_kernel, block), out_shape=(jax.S...  33.7 us
    ppermute x5, waiting for transfers between devices, halve(): lax.ppermute(give.astype(jnp.bfloat16), axis, [(i, i ^ bit) for i in rang...  28.1 us
    all_gather x1, waiting for transfers between devices, per_device(): packed = lax.all_gather(jnp.concatenate([own_rows, digits]), 'sec', axis=0)  25.2 us
    pallas_call x2, Pallas kernels, sweep(): pl.pallas_call(functools.partial(sweep_kernel, protos), out_shape=jax.Sha...  14.1 us
    pallas_call x1, Pallas kernels, target_mean(): pl.pallas_call(functools.partial(mean_kernel, protos), out_shape=(jax.Sha...  12.6 us
    unnamed x36, local copies, waits for them, and re-layouts  10.9 us
    pallas_call x1, Pallas kernels, teacher_expo(): pl.pallas_call(teacher_kernel, out_shape=(jax.ShapeDtypeStruct((count, co...  10.3 us
  transfers between devices with their start and end apart: 6, of which 6 were waited for; matrix products, arithmetic and copies ran while one was open for 0% of the time, Pallas kernels for 0%

profile of v2, /device:TPU:0, one launch (start us, length us, event | category | flops | bytes accessed | tf_op | source)
XLA Modules:
  0.0 242.8 jit_solution(16746000027948288522)
XLA Ops:
  11.4 25.2 %all-gather.3.cloned.1.call-done = bf16[2112,512]{1,0:T(8,128)(2,1)} async-done(((bf16[528,512]{1,0:T(8,128)(2,1)}), bf16[2112,512]{1,0:T(8,128)(2,1)}) %all-gather.3.cloned.1.call-update) | async-done | bytes 2162704 | tf_op jit(solution)/shard_map/all_gather | solution.py:332
  40.3 33.7 %shard_map.60 = (f32[1536,512]{1,0:T(8,128)}, f32[1536,1]{1,0:T(8,128)S(1)}, f32[1536,1]{1,0:T(8,128)S(1)}) custom-call(s32[1]{0:T(128)} %bitcast.rows_ref_sec.sec_ref, bf16[1536,512]{1,0:T(8,128)(2,1)S(1)} %bitcast.80, bf16[512,32768]{1,0:T(8,128)(2,1)} %proto_ref.5), custom_call_target="tpu_custom_call" | custom-call | flops 25769803776 | bytes 16777216 | tf_op jit(solution)/shard_map/pallas_call | solution.py:202
  74.9 10.3 %shard_map.59 = (bf16[512,8192]{1,0:T(8,128)(2,1)}, f32[4,512,1]{2,1,0:T(8,128)S(1)}) custom-call(s32[1]{0:T(128)} %bitcast.rows_ref_sec.sec_ref, bf16[512,512]{1,0:T(8,128)(2,1)S(1)} %get-tuple-element.21.rows_ref, bf16[512,32768]{1,0:T(8,128)(2,1)} %proto_ref.5), custom_call_target="tpu_custom_call" | custom-call | flops 4294967296 | bytes 16777216 | tf_op jit(solution)/shard_map/pallas_call | solution.py:44
  86.3 11.0 %shard_map.61 = f32[16,128]{1,0:T(8,128)} custom-call(f32[16,128]{1,0:T(8,128)} %maximum_bitcast_fusion.value_ref), custom_call_target="tpu_custom_call" | custom-call | tf_op jit(solution)/shard_map/pallas_call | solution.py:279
  98.7 1.4 multiply_exponential_fusion.factor_ref
  100.2 7.0 %shard_map.62 = f32[512,1]{1,0:T(8,128)S(1)} custom-call(f32[4,512,1]{2,1,0:T(8,128)S(1)} %multiply_exponential_fusion.factor_ref, f32[512,1]{1,0:T(8,128)S(1)} %broadcast.157.weight_ref, bf16[512,8192]{1,0:T(8,128)(2,1)} %get-tuple-element.11.expo_ref), custom_call_target="tpu_custom_call" | custom-call | flops 25165824 | bytes 8388608 | tf_op jit(solution)/shard_map/pallas_call | solution.py:92
  109.6 10.5 %shard_map.63 = f32[8,128]{1,0:T(8,128)} custom-call(f32[8,128]{1,0:T(8,128)} %pad_bitcast_fusion.1.value_ref), custom_call_target="tpu_custom_call" | custom-call | tf_op jit(solution)/shard_map/pallas_call | solution.py:279
  122.6 7.0 %shard_map.64 = f32[512,1]{1,0:T(8,128)S(1)} custom-call(f32[4,512,1]{2,1,0:T(8,128)S(1)} %multiply_exponential_fusion.factor_ref, f32[512,1]{1,0:T(8,128)S(1)} %copy-done.3, bf16[512,8192]{1,0:T(8,128)(2,1)} %get-tuple-element.11.expo_ref), custom_call_target="tpu_custom_call" | custom-call | flops 25165824 | bytes 8388608 | tf_op jit(solution)/shard_map/pallas_call | solution.py:92
  132.1 10.9 %shard_map.65 = f32[8,128]{1,0:T(8,128)} custom-call(f32[8,128]{1,0:T(8,128)} %pad_bitcast_fusion.value_ref), custom_call_target="tpu_custom_call" | custom-call | tf_op jit(solution)/shard_map/pallas_call | solution.py:279
  145.5 12.6 %shard_map.66 = (f32[512,512]{1,0:T(8,128)S(1)}, f32[512,1]{1,0:T(8,128)S(1)}) custom-call(s32[1]{0:T(128)} %bitcast.rows_ref_sec.sec_ref, f32[4,512,1]{2,1,0:T(8,128)S(1)} %multiply_exponential_fusion.factor_ref, f32[512,1]{1,0:T(8,128)S(1)} %copy-done.1, bf16[512,8192]{1,0:T(8,128)(2,1)} %get-tuple-element.11.expo_ref, bf16[512,32768]{1,0:T(8,128)(2,1)} %proto_ref.5), custom_call_target="tpu_custom_call" | custom-call | flops 4294967296 | bytes 16777216 | tf_op jit(solution)/shard_map/pallas_call | solution.py:133
  162.1 1.7 multiply_reduce_fusion.1
  163.8 2.7 %multiply_reduce_fusion = (f32[1536]{0:T(1024)S(1)}, f32[1536,512]{1,0:T(8,128)}) fusion(bf16[3,512,512]{2,1,0:T(8,128)(2,1)S(1)} %pad_maximum_fusion.1, f32[512,512]{1,0:T(8,128)S(1)} %copy-done.6, s32[1536]{0:T(1024)S(1)} %eq.17), kind=kOutput, calls=%fused_computation.3 | convolution fusion | flops 808712704 | bytes 5779456 | tf_op jit(solution)/shard_map/dot_general | solution.py:359
  167.2 11.6 %shard_map.67 = f32[32,128]{1,0:T(8,128)} custom-call(f32[32,128]{1,0:T(8,128)} %fusion.16.value_ref), custom_call_target="tpu_custom_call" | custom-call | tf_op jit(solution)/shard_map/pallas_call | solution.py:279
  180.3 9.5 %gather_fusion = f32[1536]{0:T(1024)S(1)} fusion(f32[512]{0:T(512)S(1)} %slice_bitcast_fusion.5, s32[2048]{0:T(1024)S(1)} %pad_clamp_fusion), kind=kCustom, calls=%fused_computation | custom fusion | bytes 18432 | tf_op jit(solution)/shard_map/jit(_take)/gather | solution.py:367
  190.4 3.5 %divide_subtract_fusion = f32[1536,512]{1,0:T(8,128)S(1)} fusion(f32[1536,512]{1,0:T(8,128)} %get-tuple-element.31, f32[1536,512]{1,0:T(8,128)} %get-tuple-element.15, f32[1536]{0:T(1024)S(1)} %and_select_fusion, f32[1536]{0:T(1024)S(1)} %fusion.7), kind=kLoop, calls=%fused_computation.2 | loop fusion | flops 2359296 | bytes 9449472 | tf_op jit(solution)/shard_map/sub | solution.py:368
  194.9 1.9 copy-done.9
  197.0 2.6 %collective-permute-done = bf16[2,512,512]{2,1,0:T(8,128)(2,1)S(1)} collective-permute-done((bf16[2,512,512]{2,1,0:T(8,128)(2,1)S(1)}, bf16[2,512,512]{2,1,0:T(8,128)(2,1)S(1)}, u32[]{:S(2)}, u32[]{:S(2)}) %collective-permute-start) | collective-permute-done | bytes 1048608 | tf_op jit(solution)/shard_map/ppermute | solution.py:305
  199.7 2.0 bitcast_add_fusion
  202.4 13.5 %collective-permute-done.1 = bf16[1,512,512]{2,1,0:T(8,128)(2,1)} collective-permute-done((bf16[1,512,512]{2,1,0:T(8,128)(2,1)S(1)}, bf16[1,512,512]{2,1,0:T(8,128)(2,1)}, u32[]{:S(2)}, u32[]{:S(2)}) %collective-permute-start.1) | collective-permute-done | bytes 524320 | tf_op jit(solution)/shard_map/ppermute | solution.py:305
  217.1 1.9 collective-permute-start.2
  219.1 5.7 %collective-permute-done.2 = bf16[4,64,512]{2,1,0:T(8,128)(2,1)S(1)} collective-permute-done((bf16[4,64,512]{2,1,0:T(8,128)(2,1)S(1)}, bf16[4,64,512]{2,1,0:T(8,128)(2,1)S(1)}, u32[]{:S(2)}, u32[]{:S(2)}) %collective-permute-start.2) | collective-permute-done | bytes 262176 | tf_op jit(solution)/shard_map/ppermute | solution.py:305
  226.7 3.2 %collective-permute-done.3 = bf16[2,64,512]{2,1,0:T(8,128)(2,1)S(1)} collective-permute-done((bf16[2,64,512]{2,1,0:T(8,128)(2,1)S(1)}, bf16[2,64,512]{2,1,0:T(8,128)(2,1)S(1)}, u32[]{:S(2)}, u32[]{:S(2)}) %collective-permute-start.3) | collective-permute-done | bytes 131104 | tf_op jit(solution)/shard_map/ppermute | solution.py:305
  230.0 2.1 collective-permute-start.4
  232.1 3.1 %collective-permute-done.4 = bf16[1,64,512]{2,1,0:T(8,128)(2,1)S(1)} collective-permute-done((bf16[1,64,512]{2,1,0:T(8,128)(2,1)S(1)}, bf16[1,64,512]{2,1,0:T(8,128)(2,1)S(1)}, u32[]{:S(2)}, u32[]{:S(2)}) %collective-permute-start.4) | collective-permute-done | bytes 65568 | tf_op jit(solution)/shard_map/ppermute | solution.py:305
  (97 shorter events, 33.6 us)
Async XLA Ops:
  7.2 29.4 %all-gather.3.cloned.1.call-start = ((), (), s32[]{:S(2)}) async-start(), calls=%async_computation | async-start | bytes 2703360 | tf_op jit(solution)/shard_map/all_gather | solution.py:332
  37.5 2.7 %copy-start.12 = (s32[4,512]{1,0:T(4,128)}, s32[4,512]{1,0:T(4,128)S(1)}, u32[]{:S(2)}) copy-start(s32[4,512]{1,0:T(4,128)S(1)} %slice_add_fusion) | copy-start | bytes 24580
  74.0 0.9 copy-start.7
  74.9 23.8 %slice-start = ((s32[4,512]{1,0:T(4,128)}), s32[2,512]{1,0:T(2,128)S(1)}, s32[]{:S(2)}) async-start(s32[4,512]{1,0:T(4,128)} %copy-done.12), calls=%async_computation.1 | async-start | bytes 8192 | tf_op jit(solution)/shard_map/slice | solution.py:338
  85.2 13.5 %copy-start = (f32[4,512,1]{2,1,0:T(8,128)}, f32[4,512,1]{2,1,0:T(8,128)S(1)}, u32[]{:S(2)}) copy-start(f32[4,512,1]{2,1,0:T(8,128)S(1)} %get-tuple-element.9) | copy-start | bytes 24580
  107.2 0.7 copy-start.2
  121.7 0.9 copy-start.3
  129.6 0.7 copy-start.4
  144.5 0.9 copy-start.1
  158.1 1.0 copy-start.5
  159.1 0.7 copy-start.8
  159.8 4.0 %copy-start.6 = (f32[512,512]{1,0:T(8,128)S(1)}, f32[512,512]{1,0:T(8,128)}, u32[]{:S(2)}) copy-start(f32[512,512]{1,0:T(8,128)} %copy-done.5) | copy-start | bytes 3145732
  163.8 15.6 %copy-start.11 = (f32[16,128]{1,0:T(8,128)S(1)}, f32[16,128]{1,0:T(8,128)}, u32[]{:S(2)}) copy-start(f32[16,128]{1,0:T(8,128)} %shard_map.61) | copy-start | bytes 24580
  180.3 9.8 %copy-start.10 = (f32[1,1536]{0,1:T(8,128)S(1)}, f32[1,1536]{0,1:T(8,128)}, u32[]{:S(2)}) copy-start(f32[1,1536]{0,1:T(8,128)} %copy.22) | copy-start | bytes 18436
  194.9 1.9 copy-start.9
  196.9 2.7 %collective-permute-start = (bf16[2,512,512]{2,1,0:T(8,128)(2,1)S(1)}, bf16[2,512,512]{2,1,0:T(8,128)(2,1)S(1)}, u32[]{:S(2)}, u32[]{:S(2)}) collective-permute-start(bf16[2,512,512]{2,1,0:T(8,128)(2,1)S(1)} %fusion.4), channel_id=1, source_target_pairs={{0,8},{8,0},{16,24},{24,16},{1,9},{9,1},{17,25},{25,17},{2,10},{10... | collective-permute-start | bytes 3145736 | tf_op jit(solution)/shard_map/ppermute | solution.py:305
  201.6 24.5 %copy-start.13 = (s32[512]{0:T(512)S(1)}, s32[512]{0:T(512)}, u32[]{:S(2)}) copy-start(s32[512]{0:T(512)} %param.7) | copy-start | bytes 6148
  201.7 14.1 %collective-permute-start.1 = (bf16[1,512,512]{2,1,0:T(8,128)(2,1)S(1)}, bf16[1,512,512]{2,1,0:T(8,128)(2,1)}, u32[]{:S(2)}, u32[]{:S(2)}) collective-permute-start(bf16[1,512,512]{2,1,0:T(8,128)(2,1)S(1)} %dynamic-slice_convert_fusion.1), channel_id=1, source_target_pairs={{0,16},{8,24},{16,0},{24,8},{1,17},{9,25},{17,1},{25,9},{2,18},{10... | collective-permute-start | bytes 1572872 | tf_op jit(solution)/shard_map/ppermute | solution.py:305
  217.1 7.7 %collective-permute-start.2 = (bf16[4,64,512]{2,1,0:T(8,128)(2,1)S(1)}, bf16[4,64,512]{2,1,0:T(8,128)(2,1)S(1)}, u32[]{:S(2)}, u32[]{:S(2)}) collective-permute-start(bf16[4,64,512]{2,1,0:T(8,128)(2,1)S(1)} %fusion.9), channel_id=1, source_target_pairs={{0,1},{1,0},{2,3},{3,2},{4,5},{5,4},{6,7},{7,6},{8,9},{9,8},{10,11... | collective-permute-start | bytes 786440 | tf_op jit(solution)/shard_map/ppermute | solution.py:305
  224.9 5.0 %collective-permute-start.3 = (bf16[2,64,512]{2,1,0:T(8,128)(2,1)S(1)}, bf16[2,64,512]{2,1,0:T(8,128)(2,1)S(1)}, u32[]{:S(2)}, u32[]{:S(2)}) collective-permute-start(bf16[2,64,512]{2,1,0:T(8,128)(2,1)S(1)} %fusion.10), channel_id=1, source_target_pairs={{0,2},{1,3},{2,0},{3,1},{4,6},{5,7},{6,4},{7,5},{8,10},{9,11},{10,... | collective-permute-start | bytes 393224 | tf_op jit(solution)/shard_map/ppermute | solution.py:305
  230.0 5.2 %collective-permute-start.4 = (bf16[1,64,512]{2,1,0:T(8,128)(2,1)S(1)}, bf16[1,64,512]{2,1,0:T(8,128)(2,1)S(1)}, u32[]{:S(2)}, u32[]{:S(2)}) collective-permute-start(bf16[1,64,512]{2,1,0:T(8,128)(2,1)S(1)} %dynamic-slice_convert_fusion.4), channel_id=1, source_target_pairs={{0,4},{1,5},{2,6},{3,7},{4,0},{5,1},{6,2},{7,3},{8,12},{9,13},{10,... | collective-permute-start | bytes 196616 | tf_op jit(solution)/shard_map/ppermute | solution.py:305
Sparse Core Ops, SparseCore 0:
  11.4 25.1 all-gather.2

commit v3 on v2

--- a/solution.py
+++ b/solution.py
@@ -158,156 +158,238 @@
     )(sec_index, factor, weight, expo_tab, prototypes)
 
 
-def student_kernel(block, sec_ref, rows_ref, proto_ref, grad_ref, top_ref, total_ref, partial):
+def fold(combine):
+    def run(values):
+        total = values[0]
+        for value in values[1:]:
+            total = combine(total, value)
+        return total
+
+    return run
+
+
+def fold_softmax(top_rows):
+    def run(values):
+        tops = [value[:top_rows] for value in values]
+        highest = fold(jnp.maximum)(tops)
+        totals = fold(jnp.add)(
+            [
+                value[top_rows : 2 * top_rows] * jnp.exp2((top - highest) * (LOG2E / STUD_TEMP))
+                for value, top in zip(values, tops)
+            ]
+        )
+        return jnp.concatenate(
+            [highest, totals, fold(jnp.add)([value[2 * top_rows :] for value in values])]
+        )
+
+    return run
+
+
+class Exchange:
+    def __init__(self, sizes, combine, slots, send_sems, recv_sems):
+        self.sizes, self.combine, self.slots = sizes, combine, slots
+        self.send_sems, self.recv_sems = send_sems, recv_sems
+
+    def greet(self):
+        barrier = pltpu.get_barrier_semaphore()
+        for axis, size in zip(AXES, self.sizes):
+            me = lax.axis_index(axis)
+            for shift in range(1, size):
+                pl.semaphore_signal(
+                    barrier,
+                    inc=1,
+                    device_id={axis: lax.rem(me + shift, size)},
+                    device_id_type=pl.DeviceIdType.MESH,
+                )
+
+    def wait_greetings(self):
+        pl.semaphore_wait(pltpu.get_barrier_semaphore(), sum(self.sizes) - len(self.sizes))
+
+    def copies(self, turn):
+        size = self.sizes[turn]
+        me = lax.axis_index(AXES[turn])
+        first = sum(self.sizes[:turn]) - turn
+        return [
+            pltpu.make_async_remote_copy(
+                src_ref=self.slots[turn].at[me],
+                dst_ref=self.slots[turn].at[me],
+                send_sem=self.send_sems.at[first + shift - 1],
+                recv_sem=self.recv_sems.at[first + shift - 1],
+                device_id={AXES[turn]: lax.rem(me + shift, size)},
+                device_id_type=pl.DeviceIdType.MESH,
+            )
+            for shift in range(1, size)
+        ]
+
+    def send(self, turn, value):
+        self.slots[turn][lax.axis_index(AXES[turn])] = value
+        for copy in self.copies(turn):
+            copy.start()
+
+    def collect(self, turn):
+        for copy in self.copies(turn):
+            copy.wait()
+        return self.combine([self.slots[turn][other] for other in range(self.sizes[turn])])
+
+
+def exchange_scratch(sizes, rows):
+    peers = sum(sizes) - len(sizes)
+    return [pltpu.VMEM((size, rows, 128), jnp.float32) for size in sizes] + [
+        pltpu.SemaphoreType.DMA((peers,)),
+        pltpu.SemaphoreType.DMA((peers,)),
+    ]
+
+
+def pack(vectors):
+    pieces = []
+    for vector in vectors:
+        flat = vector.reshape(-1)
+        pieces.append(jnp.pad(flat, (0, -flat.shape[0] % 1024)).reshape(-1, 128))
+    return jnp.concatenate(pieces)
+
+
+def unpack(shared, vectors):
+    results, at = [], 0
+    for vector in vectors:
+        rows = -(-vector.size // 1024) * 8
+        flat = shared[at : at + rows].reshape(-1)[: vector.size]
+        results.append(flat.reshape(vector.shape))
+        at += rows
+    return results
+
+
+def share_kernel(sizes, combine, value_ref, out_ref, sec_slot, proto_slot, send_sems, recv_sems):
+    exchange = Exchange(sizes, combine, (sec_slot, proto_slot), send_sems, recv_sems)
+    exchange.greet()
+    exchange.wait_greetings()
+    exchange.send(0, value_ref[...])
+    exchange.send(1, exchange.collect(0))
+    out_ref[...] = exchange.collect(1)
+
+
+def share(combine, vectors, collective_id):
+    sizes = tuple(lax.axis_size(axis) for axis in AXES)
+    packed = pack(vectors)
+    shared = pl.pallas_call(
+        functools.partial(share_kernel, sizes, combine),
+        out_shape=jax.ShapeDtypeStruct(packed.shape, jnp.float32),
+        in_specs=[pl.BlockSpec(memory_space=pltpu.VMEM)],
+        out_specs=pl.BlockSpec(memory_space=pltpu.VMEM),
+        scratch_shapes=exchange_scratch(sizes, packed.shape[0]),
+        compiler_params=pltpu.CompilerParams(collective_id=collective_id, has_side_effects=True),
+    )(packed)
+    return unpack(shared, vectors)
+
+
+def student_kernel(
+    steps, unit, sizes, combine,
+    rows_ref, value_ref, proto_ref,
+    grad_ref, top_ref, total_ref, shared_ref,
+    partial, sec_slot, proto_slot, send_sems, recv_sems,
+):
     step = pl.program_id(0)
+    exchange = Exchange(sizes, combine, (sec_slot, proto_slot), send_sems, recv_sems)
 
     @pl.when(step == 0)
     def _():
+        exchange.greet()
         top_ref[...] = jnp.full_like(top_ref, LOW)
         partial[...] = jnp.zeros_like(partial)
         grad_ref[...] = jnp.zeros_like(grad_ref)
 
+    @pl.when(step == min(1, steps - 1))
+    def _():
+        exchange.wait_greetings()
+        exchange.send(0, value_ref[...])
+
+    @pl.when(step == min(2, steps - 1))
+    def _():
+        exchange.send(1, exchange.collect(0))
+
     def dots_of(at):
         return jnp.dot(
-            rows_ref[at : at + block], proto_ref[...], preferred_element_type=jnp.float32
-        )
-
-    starts = list(range(0, rows_ref.shape[0], block))
+            rows_ref[...], proto_ref[:, at : at + unit], preferred_element_type=jnp.float32
+        )
+
+    starts = list(range(0, proto_ref.shape[1], unit))
     ahead = dots_of(starts[0])
     for turn, at in enumerate(starts):
         dots = ahead
         if turn + 1 < len(starts):
             ahead = dots_of(starts[turn + 1])
-        old_top = top_ref[at : at + block]
+        old_top = top_ref[...]
         new_top = jnp.maximum(old_top, jnp.max(dots, axis=1, keepdims=True))
         expo = jnp.exp2((dots - new_top) * (LOG2E / STUD_TEMP))
         shrink = jnp.exp2((old_top - new_top) * (LOG2E / STUD_TEMP))
-        top_ref[at : at + block] = new_top
-        partial[at : at + block] = partial[at : at + block] * shrink + lanes_sum(expo)
-        grad_ref[at : at + block] = grad_ref[at : at + block] * shrink + lax.dot_general(
+        top_ref[...] = new_top
+        partial[...] = partial[...] * shrink + lanes_sum(expo)
+        grad_ref[...] = grad_ref[...] * shrink + lax.dot_general(
             expo.astype(jnp.bfloat16),
-            proto_ref[...],
+            proto_ref[:, at : at + unit],
             (((1,), (1,)), ((), ())),
             preferred_element_type=jnp.float32,
         )
 
-    @pl.when(step == pl.num_programs(0) - 1)
+    @pl.when(step == steps - 1)
     def _():
         total_ref[...] = jnp.sum(partial[...], axis=1, keepdims=True)
-
-
-def student_mean(sec_index, rows, prototypes, cols, chunk, block):
+        shared_ref[...] = exchange.collect(1)
+
+
+def student_mean(rows, prototypes, cols, chunk, combine, vectors, collective_id):
     count, width = rows.shape
     steps = cols // chunk
-    return pl.pallas_call(
-        functools.partial(student_kernel, block),
+    sizes = tuple(lax.axis_size(axis) for axis in AXES)
+    packed = pack(vectors)
+    part, top, total, shared = pl.pallas_call(
+        functools.partial(student_kernel, steps, math.gcd(chunk, 1024), sizes, combine),
         out_shape=(
             jax.ShapeDtypeStruct((count, width), jnp.float32),
             jax.ShapeDtypeStruct((count, 1), jnp.float32),
             jax.ShapeDtypeStruct((count, 1), jnp.float32),
-        ),
-        grid_spec=pltpu.PrefetchScalarGridSpec(
-            num_scalar_prefetch=1,
-            grid=(steps,),
-            in_specs=[
-                pl.BlockSpec((count, width), lambda s, sec: (0, 0)),
-                pl.BlockSpec((width, chunk), lambda s, sec: (0, sec[0] * steps + s)),
-            ],
-            out_specs=[
-                pl.BlockSpec((count, width), lambda s, sec: (0, 0)),
-                pl.BlockSpec((count, 1), lambda s, sec: (0, 0)),
-                pl.BlockSpec((count, 1), lambda s, sec: (0, 0)),
-            ],
-            scratch_shapes=[pltpu.VMEM((count, 128), jnp.float32)],
-        ),
-        compiler_params=pltpu.CompilerParams(vmem_limit_bytes=VMEM_LIMIT),
+            jax.ShapeDtypeStruct(packed.shape, jnp.float32),
+        ),
+        grid=(steps,),
+        in_specs=[
+            pl.BlockSpec((count, width), lambda s: (0, 0)),
+            pl.BlockSpec(packed.shape, lambda s: (0, 0)),
+            pl.BlockSpec((width, chunk), lambda s: (0, lax.axis_index("sec") * steps + s)),
+        ],
+        out_specs=[
+            pl.BlockSpec((count, width), lambda s: (0, 0)),
+            pl.BlockSpec((count, 1), lambda s: (0, 0)),
+            pl.BlockSpec((count, 1), lambda s: (0, 0)),
+            pl.BlockSpec(packed.shape, lambda s: (0, 0)),
+        ],
+        scratch_shapes=[pltpu.VMEM((count, 128), jnp.float32)]
+        + exchange_scratch(sizes, packed.shape[0]),
+        compiler_params=pltpu.CompilerParams(
+            vmem_limit_bytes=VMEM_LIMIT, collective_id=collective_id, has_side_effects=True
+        ),
         cost_estimate=pl.CostEstimate(
             flops=4 * count * width * cols, bytes_accessed=4 * width * cols, transcendentals=0
         ),
-    )(sec_index, rows, prototypes)
-
-
-def share_kernel(combine, sizes, value_ref, out_ref, *scratch):
-    slots = scratch[: len(AXES)]
-    send_sems, recv_sems = scratch[len(AXES) :]
-    barrier = pltpu.get_barrier_semaphore()
-    peers = 0
-    for axis, size in zip(AXES, sizes):
-        me = lax.axis_index(axis)
-        for shift in range(1, size):
-            pl.semaphore_signal(
-                barrier,
-                inc=1,
-                device_id={axis: lax.rem(me + shift, size)},
-                device_id_type=pl.DeviceIdType.MESH,
-            )
-            peers += 1
-    pl.semaphore_wait(barrier, peers)
-    current = value_ref[...]
-    number = 0
-    for axis, size, slot in zip(AXES, sizes, slots):
-        me = lax.axis_index(axis)
-        slot[me] = current
-        copies = []
-        for shift in range(1, size):
-            copy = pltpu.make_async_remote_copy(
-                src_ref=slot.at[me],
-                dst_ref=slot.at[me],
-                send_sem=send_sems.at[number],
-                recv_sem=recv_sems.at[number],
-                device_id={axis: lax.rem(me + shift, size)},
-                device_id_type=pl.DeviceIdType.MESH,
-            )
-            copy.start()
-            copies.append(copy)
-            number += 1
-        for copy in copies:
-            copy.wait()
-        current = slot[0]
-        for other in range(1, size):
-            current = combine(current, slot[other])
-    out_ref[...] = current
-
-
-def share(combine, vectors, collective_id):
-    sizes = tuple(lax.axis_size(axis) for axis in AXES)
-    flat = jnp.concatenate([vector.reshape(-1) for vector in vectors])
-    count = flat.shape[0]
-    rows = -(-count // 1024) * 8
-    flat = jnp.pad(flat, (0, rows * 128 - count)).reshape(rows, 128)
-    peers = sum(sizes) - len(sizes)
-    shared = pl.pallas_call(
-        functools.partial(share_kernel, combine, sizes),
-        out_shape=jax.ShapeDtypeStruct((rows, 128), jnp.float32),
-        in_specs=[pl.BlockSpec(memory_space=pltpu.VMEM)],
-        out_specs=pl.BlockSpec(memory_space=pltpu.VMEM),
-        scratch_shapes=[pltpu.VMEM((size, rows, 128), jnp.float32) for size in sizes]
-        + [pltpu.SemaphoreType.DMA((peers,)), pltpu.SemaphoreType.DMA((peers,))],
-        compiler_params=pltpu.CompilerParams(collective_id=collective_id, has_side_effects=True),
-    )(flat).reshape(-1)
-    results, at = [], 0
-    for vector in vectors:
-        results.append(shared[at : at + vector.size].reshape(vector.shape))
-        at += vector.size
-    return results
-
-
-def halve(blocks, axis):
-    size = lax.axis_size(axis)
-    index = lax.axis_index(axis)
-    bit = 1
-    while bit < size:
-        rows, width = blocks.shape[1:]
-        pairs = blocks.reshape(-1, 2, rows, width)
-        mine = lax.rem(index // bit, 2)
-        keep = lax.dynamic_index_in_dim(pairs, mine, 1, keepdims=False)
-        give = lax.dynamic_index_in_dim(pairs, 1 - mine, 1, keepdims=False)
+    )(rows, packed, prototypes)
+    return part, top, total, unpack(shared, vectors)
+
+
+def halve(blocks, order):
+    for axis, bit in order:
+        size, dim = lax.axis_size(axis), AXES.index(axis)
+        mine = lax.rem(lax.axis_index(axis) // bit, 2)
+        shape = blocks.shape
+        pairs = blocks.reshape(shape[:dim] + (shape[dim] // 2, 2) + shape[dim + 1 :])
+        keep = lax.dynamic_index_in_dim(pairs, mine, dim + 1, keepdims=False)
+        give = lax.dynamic_index_in_dim(pairs, 1 - mine, dim + 1, keepdims=False)
         got = lax.ppermute(
             give.astype(jnp.bfloat16), axis, [(i, i ^ bit) for i in range(size)]
         )
         blocks = keep + got.astype(jnp.float32)
-        bit *= 2
-    return blocks[0]
+    return blocks[0, 0]
+
+
+def bits_of(axis):
+    return [(axis, 1 << at) for at in range(lax.axis_size(axis).bit_length() - 1)]
 
 
 def per_device(features, prototypes, crop_sample, crop_live):
@@ -341,17 +423,24 @@
     stud_samples = students_of(all_samples).reshape(-1)
     teach_rows = all_rows[first_dev : first_dev + teach_devs].reshape(-1, width)
 
-    stud_part, stud_top, stud_total = student_mean(
-        sec_array, stud_rows, prototypes, cols, chunk, row_count
-    )
     expo_tab, chunk_tops = teacher_expo(sec_array, teach_rows, prototypes, cols, chunk)
-    row_top, global_top = share(jnp.maximum, [jnp.max(chunk_tops, axis=0), stud_top], 0)
+    groups = stud_rows.reshape(ITERS, -1, width)
+    found = []
+    top_part = jnp.max(chunk_tops, axis=0)
+    part, top, total, (row_top,) = student_mean(
+        groups[0], prototypes, cols, chunk, fold(jnp.maximum), [top_part], 0
+    )
+    found.append((part, top, total))
     factor = jnp.exp2((chunk_tops - row_top) * (LOG2E / TEACH_TEMP))
     weight = jnp.ones_like(row_top)
-    for turn in range(ITERS - 1):
+    for turn in range(1, ITERS):
         row_part = sweep(factor, weight, expo_tab, protos, chunk)
-        (row_total,) = share(jnp.add, [row_part], 1 + turn)
+        part, top, total, (row_total,) = student_mean(
+            groups[turn], prototypes, cols, chunk, fold(jnp.add), [row_part], turn
+        )
+        found.append((part, top, total))
         weight = 1.0 / (sample_count * row_total)
+    stud_part, stud_top, stud_total = [jnp.concatenate(pieces) for pieces in zip(*found)]
     target_part, target_total = target_mean(
         sec_array, factor, weight, expo_tab, prototypes, protos, chunk
     )
@@ -360,17 +449,26 @@
         pick, target_part.astype(jnp.bfloat16), preferred_element_type=jnp.float32
     )
     cross_part = jnp.sum(stud_rows.astype(jnp.float32) * chosen_part, axis=1, keepdims=True)
+    global_top, stud_total, target_total, cross = share(
+        fold_softmax(-(-stud_top.size // 1024) * 8),
+        [stud_top, stud_total, target_total, cross_part],
+        ITERS,
+    )
     shrink = jnp.exp2((stud_top - global_top) * (LOG2E / STUD_TEMP))
-    target_total, stud_total, cross = share(
-        jnp.add, [target_total, stud_total * shrink, cross_part], ITERS
-    )
-    chosen_total = jnp.take(target_total[:, 0], stud_samples)[:, None]
+    chosen_total = jnp.sum(
+        jnp.where(pick > 0, target_total.reshape(1, -1), 0.0), axis=1, keepdims=True
+    )
     gap_part = stud_part * (shrink / stud_total) - chosen_part / chosen_total
     gap_part = gap_part.reshape(-1, row_count, width)
     blank = jnp.zeros((teach_devs, row_count, width), jnp.float32)
     blocks = jnp.concatenate([gap_part[:first_dev], blank, gap_part[first_dev:]])
-    block = halve(blocks, "sec")
-    gap = halve(block.reshape(proto_devs, row_count // proto_devs, width), "proto")
+    blocks = blocks.reshape(sec_devs, proto_devs, row_count // proto_devs, width)
+    over_sec, over_proto = bits_of("sec"), bits_of("proto")
+    one = halve(blocks[..., : width // 2], over_sec + over_proto)
+    two = halve(
+        blocks[..., width // 2 :], over_sec[:1] + over_proto[:1] + over_sec[1:] + over_proto[1:]
+    )
+    gap = jnp.concatenate([one, two], axis=1)
 
     loss = global_top / STUD_TEMP + jnp.log(stud_total) - cross / chosen_total / STUD_TEMP
     place = jnp.where(sec_index < first_dev, sec_index, sec_index - teach_devs)

time: 244 us -> 186 us (0.76)
  Pallas kernels: 115 us -> 90.4 us
  waiting for transfers between devices: 53.4 us -> 36.6 us
  local copies, waits for them, and re-layouts: 28 us -> 12.2 us
  other arithmetic: 23.6 us -> 14.3 us
  starting transfers between devices: 5.94 us -> 14.1 us
    pallas_call x5 -> x4, Pallas kernels: 77.7 us -> 53.2 us  [the longest x3 40.9 us: student_mean(): pl.pallas_call(functools.partial(student_kernel, steps, math.gcd(chunk, 1...]
    ppermute x5 -> x10, waiting for transfers between devices: 28.1 us -> 11.5 us  [halve(): lax.ppermute(give.astype(jnp.bfloat16), axis, [(i, i ^ bit) for i in rang...]
    gather x2 -> x0, local copies, waits for them, and re-layouts: 9.49 us -> none  [per_device(): chosen_total = jnp.take(target_total[:, 0], stud_samples)[:, None]]
    ppermute x5 -> x10, starting transfers between devices: 5.9 us -> 14.1 us  [halve(): lax.ppermute(give.astype(jnp.bfloat16), axis, [(i, i ^ bit) for i in rang...]
    unnamed x36 -> x32, local copies, waits for them, and re-layouts: 10.9 us -> 5.77 us
    add x4 -> x8, other arithmetic: 3.27 us -> 0.45 us  [halve(): blocks = keep + got.astype(jnp.float32)]
  transfers between devices with their start and end apart: 6 -> 11, of which waited for: 6 -> 9; matrix products, arithmetic and copies ran while one was open for 0% -> 1% of each run, Pallas kernels for 0% -> 0%
where the time goes in v3:
time: 186 us; the launch traced here: 185 us
  Pallas kernels  90.4 us (49%)
  waiting for transfers between devices  36.6 us (20%)
  between operations  14.7 us (8%)
  other arithmetic  14.3 us (8%)
  starting transfers between devices  14.1 us (8%)
  local copies, waits for them, and re-layouts  12.2 us (7%)
  matrix products  2.79 us (2%)
    pallas_call x3, Pallas kernels, student_mean(): pl.pallas_call(functools.partial(student_kernel, steps, math.gcd(chunk, 1...  40.9 us
    all_gather x1, waiting for transfers between devices, per_device(): packed = lax.all_gather(jnp.concatenate([own_rows, digits]), 'sec', axis=0)  25.1 us
    ppermute x10, starting transfers between devices, halve(): lax.ppermute(give.astype(jnp.bfloat16), axis, [(i, i ^ bit) for i in rang...  14.1 us
    pallas_call x2, Pallas kernels, sweep(): pl.pallas_call(functools.partial(sweep_kernel, protos), out_shape=jax.Sha...  14.1 us
    pallas_call x1, Pallas kernels, target_mean(): pl.pallas_call(functools.partial(mean_kernel, protos), out_shape=(jax.Sha...  12.8 us
    pallas_call x1, Pallas kernels, share(): pl.pallas_call(functools.partial(share_kernel, sizes, combine), out_shape...  12.3 us
    ppermute x10, waiting for transfers between devices, halve(): lax.ppermute(give.astype(jnp.bfloat16), axis, [(i, i ^ bit) for i in rang...  11.5 us
    pallas_call x1, Pallas kernels, teacher_expo(): pl.pallas_call(teacher_kernel, out_shape=(jax.ShapeDtypeStruct((count, co...  10.3 us
  transfers between devices with their start and end apart: 11, of which 9 were waited for; matrix products, arithmetic and copies ran while one was open for 1% of the time, Pallas kernels for 0%

profile of v3, /device:TPU:0, one launch (start us, length us, event | category | flops | bytes accessed | tf_op | source)
XLA Modules:
  0.0 185.1 jit_solution(802242389188311126)
XLA Ops:
  7.2 1.2 fusion.5
  11.5 25.1 %all-gather.3.cloned.1.call-done = bf16[2112,512]{1,0:T(8,128)(2,1)} async-done(((bf16[528,512]{1,0:T(8,128)(2,1)}), bf16[2112,512]{1,0:T(8,128)(2,1)}) %all-gather.3.cloned.1.call-update) | async-done | bytes 2162704 | tf_op jit(solution)/shard_map/all_gather | solution.py:414
  37.7 2.3 %slice.115 = bf16[2,512,512]{2,1,0:T(8,128)(2,1)} slice(bf16[4,528,512]{2,1,0:T(8,128)(2,1)} %bitcast.88), slice={[0:2], [0:512], [0:512]} | slice | bytes 2097152 | tf_op jit(solution)/shard_map/slice | solution.py:420
  41.1 10.3 %shard_map.59 = (bf16[512,8192]{1,0:T(8,128)(2,1)}, f32[4,512,1]{2,1,0:T(8,128)S(1)}) custom-call(s32[1]{0:T(128)} %bitcast.2.rows_ref_sec.sec_ref, bf16[512,512]{1,0:T(8,128)(2,1)S(1)} %get-tuple-element.43.rows_ref, bf16[512,32768]{1,0:T(8,128)(2,1)} %proto_ref.9), custom_call_target="tpu_custom_call" | custom-call | flops 4294967296 | bytes 16777216 | tf_op jit(solution)/shard_map/pallas_call | solution.py:44
  51.5 14.4 %shard_map.60 = (f32[512,512]{1,0:T(8,128)S(1)}, f32[512,1]{1,0:T(8,128)S(1)}, f32[512,1]{1,0:T(8,128)S(1)}, f32[8,128]{1,0:T(8,128)S(1)}) custom-call(bf16[512,512]{1,0:T(8,128)(2,1)S(1)} %get-tuple-element.44.rows_ref, f32[8,128]{1,0:T(8,128)S(1)} %pad_bitcast_fusion.6.value_ref, bf16[512,32768]{1,0:T(8,128)(2,1)} %proto_ref.9), custom_call_target="tpu_custom_call" | custom-call | flops 8589934592 | bytes 16777216 | tf_op jit(solution)/shard_map/pallas_call | solution.py:344
  67.3 7.0 %shard_map.61 = f32[512,1]{1,0:T(8,128)S(1)} custom-call(f32[4,512,1]{2,1,0:T(8,128)S(1)} %multiply_exponential_fusion.factor_ref, f32[512,1]{1,0:T(8,128)S(1)} %broadcast_7_weight_ref.2.weight_ref, bf16[512,8192]{1,0:T(8,128)(2,1)} %get-tuple-element.21.expo_ref), custom_call_target="tpu_custom_call" | custom-call | flops 25165824 | bytes 8388608 | tf_op jit(solution)/shard_map/pallas_call | solution.py:92
  74.5 13.3 %shard_map.62 = (f32[512,512]{1,0:T(8,128)S(1)}, f32[512,1]{1,0:T(8,128)S(1)}, f32[512,1]{1,0:T(8,128)S(1)}, f32[8,128]{1,0:T(8,128)S(1)}) custom-call(bf16[512,512]{1,0:T(8,128)(2,1)S(1)} %get-tuple-element.42.rows_ref, f32[8,128]{1,0:T(8,128)S(1)} %pad_bitcast_fusion.5.value_ref, bf16[512,32768]{1,0:T(8,128)(2,1)} %proto_ref.9), custom_call_target="tpu_custom_call" | custom-call | flops 8589934592 | bytes 16777216 | tf_op jit(solution)/shard_map/pallas_call | solution.py:344
  89.2 7.0 %shard_map.63 = f32[512,1]{1,0:T(8,128)S(1)} custom-call(f32[4,512,1]{2,1,0:T(8,128)S(1)} %multiply_exponential_fusion.factor_ref, f32[512,1]{1,0:T(8,128)S(1)} %copy.25.weight_ref, bf16[512,8192]{1,0:T(8,128)(2,1)} %get-tuple-element.21.expo_ref), custom_call_target="tpu_custom_call" | custom-call | flops 25165824 | bytes 8388608 | tf_op jit(solution)/shard_map/pallas_call | solution.py:92
  96.4 13.2 %shard_map.64 = (f32[512,512]{1,0:T(8,128)S(1)}, f32[512,1]{1,0:T(8,128)S(1)}, f32[512,1]{1,0:T(8,128)S(1)}, f32[8,128]{1,0:T(8,128)S(1)}) custom-call(bf16[512,512]{1,0:T(8,128)(2,1)S(1)} %get-tuple-element.41.rows_ref, f32[8,128]{1,0:T(8,128)S(1)} %pad_bitcast_fusion.4.value_ref, bf16[512,32768]{1,0:T(8,128)(2,1)} %proto_ref.9), custom_call_target="tpu_custom_call" | custom-call | flops 8589934592 | bytes 16777216 | tf_op jit(solution)/shard_map/pallas_call | solution.py:344
  111.5 12.8 %shard_map.65 = (f32[512,512]{1,0:T(8,128)S(1)}, f32[512,1]{1,0:T(8,128)S(1)}) custom-call(s32[1]{0:T(128)} %bitcast.2.rows_ref_sec.sec_ref, f32[4,512,1]{2,1,0:T(8,128)S(1)} %multiply_exponential_fusion.factor_ref, f32[512,1]{1,0:T(8,128)S(1)} %copy.32.weight_ref, bf16[512,8192]{1,0:T(8,128)(2,1)} %get-tuple-element.21.expo_ref, bf16[512,32768]{1,0:T(8,128)(2,1)} %proto_ref.9), custom_call_target="tpu_custom_call" | custom-call | flops 4294967296 | bytes 16777216 | tf_op jit(solution)/shard_map/pallas_call | solution.py:133
  126.6 2.8 %fusion.1 = (f32[1536]{0:T(1024)S(1)}, f32[1536,512]{1,0:T(8,128)}) fusion(bf16[3,512,512]{2,1,0:T(8,128)(2,1)S(1)} %pad_maximum_fusion.1, f32[512,512]{1,0:T(8,128)S(1)} %copy-done.7, s32[1536]{0:T(1024)S(1)} %eq.17), kind=kOutput, calls=%fused_computation.4 | convolution fusion | flops 808712704 | bytes 5779456 | tf_op jit(solution)/shard_map/dot_general | solution.py:448
  130.0 12.3 %shard_map.66 = f32[56,128]{1,0:T(8,128)} custom-call(f32[56,128]{1,0:T(8,128)} %pad_maximum_fusion.3.value_ref), custom_call_target="tpu_custom_call" | custom-call | tf_op jit(solution)/shard_map/pallas_call | solution.py:273
  145.3 3.3 %fusion = f32[1536,512]{1,0:T(8,128)S(1)} fusion(f32[512,512]{1,0:T(8,128)S(1)} %copy-done.5, f32[512,512]{1,0:T(8,128)S(1)} %copy-done.3, f32[512,512]{1,0:T(8,128)S(1)} %copy-done.1, f32[1536,512]{1,0:T(8,128)} %get-tuple-element.50, f32[1536]{0:T(1024)S(1)} %select_reduce_fusion, f32[1536]{0:T(1024)S(1)} %fusion.21), kind=kLoop, calls=%fused_computation.2 | loop fusion | flops 3932160 | bytes 9449472 | tf_op jit(solution)/shard_map/sub | solution.py:461
  152.5 1.3 collective-permute-start.1
  154.0 2.0 %collective-permute-start.6 = (bf16[2,4,64,256]{3,2,1,0:T(8,128)(2,1)S(1)}, bf16[2,4,64,256]{3,2,1,0:T(8,128)(2,1)S(1)}, u32[]{:S(2)}, u32[]{:S(2)}) collective-permute-start(bf16[2,4,64,256]{3,2,1,0:T(8,128)(2,1)S(1)} %fusion.10), channel_id=1, source_target_pairs={{0,1},{1,0},{2,3},{3,2},{4,5},{5,4},{6,7},{7,6},{8,9},{9,8},{10,11... | collective-permute-start | bytes 786440 | tf_op jit(solution)/shard_map/ppermute | solution.py:384
  155.9 5.0 %collective-permute-done.1 = bf16[1,8,64,256]{3,2,1,0:T(8,128)(2,1)S(1)} collective-permute-done((bf16[1,8,64,256]{3,2,1,0:T(8,128)(2,1)S(1)}, bf16[1,8,64,256]{3,2,1,0:T(8,128)(2,1)S(1)}, u32[]{:S(2)}, u32[]{:S(2)}) %collective-permute-start.1) | collective-permute-done | bytes 262176 | tf_op jit(solution)/shard_map/ppermute | solution.py:384
  161.0 2.0 %collective-permute-start.2 = (bf16[1,4,64,256]{3,2,1,0:T(8,128)(2,1)S(1)}, bf16[1,4,64,256]{3,2,1,0:T(8,128)(2,1)S(1)}, u32[]{:S(2)}, u32[]{:S(2)}) collective-permute-start(bf16[1,4,64,256]{3,2,1,0:T(8,128)(2,1)S(1)} %fusion.11), channel_id=1, source_target_pairs={{0,1},{1,0},{2,3},{3,2},{4,5},{5,4},{6,7},{7,6},{8,9},{9,8},{10,11... | collective-permute-start | bytes 393224 | tf_op jit(solution)/shard_map/ppermute | solution.py:384
  163.1 1.3 collective-permute-start.7
  164.4 1.7 collective-permute-done.2
  166.1 2.0 %collective-permute-start.3 = (bf16[1,2,64,256]{3,2,1,0:T(8,128)(2,1)S(1)}, bf16[1,2,64,256]{3,2,1,0:T(8,128)(2,1)S(1)}, u32[]{:S(2)}, u32[]{:S(2)}) collective-permute-start(bf16[1,2,64,256]{3,2,1,0:T(8,128)(2,1)S(1)} %fusion.14), channel_id=1, source_target_pairs={{0,2},{1,3},{2,0},{3,1},{4,6},{5,7},{6,4},{7,5},{8,10},{9,11},{10,... | collective-permute-start | bytes 196616 | tf_op jit(solution)/shard_map/ppermute | solution.py:384
  168.2 1.4 collective-permute-start.8
  170.5 1.8 collective-permute-start.4
  172.6 1.8 collective-permute-start.9
  175.4 2.1 %collective-permute-done.9 = bf16[1,1,64,256]{3,2,1,0:T(8,128)(2,1)S(1)} collective-permute-done((bf16[1,1,64,256]{3,2,1,0:T(8,128)(2,1)S(1)}, bf16[1,1,64,256]{3,2,1,0:T(8,128)(2,1)S(1)}, u32[]{:S(2)}, u32[]{:S(2)}) %collective-permute-start.9) | collective-permute-done | bytes 32800 | tf_op jit(solution)/shard_map/ppermute | solution.py:384
  (123 shorter events, 23.0 us)
Async XLA Ops:
  7.2 29.4 %all-gather.3.cloned.1.call-start = ((), (), s32[]{:S(2)}) async-start(), calls=%async_computation | async-start | bytes 2703360 | tf_op jit(solution)/shard_map/all_gather | solution.py:414
  36.6 3.4 %copy-start.10 = (bf16[2112,512]{1,0:T(8,128)(2,1)S(1)}, bf16[2112,512]{1,0:T(8,128)(2,1)}, u32[]{:S(2)}) copy-start(bf16[2112,512]{1,0:T(8,128)(2,1)} %all-gather.3.cloned.1.call-done) | copy-start | bytes 6488068
  37.7 3.4 %copy-start.13 = (s32[4,512]{1,0:T(4,128)}, s32[4,512]{1,0:T(4,128)S(1)}, u32[]{:S(2)}) copy-start(s32[4,512]{1,0:T(4,128)S(1)} %slice_add_fusion) | copy-start | bytes 24580
  66.0 1.0 copy-start
  66.0 1.0 copy-start.8
  96.4 14.5 %slice-start = ((s32[4,512]{1,0:T(4,128)}), s32[2,512]{1,0:T(2,128)S(1)}, s32[]{:S(2)}) async-start(s32[4,512]{1,0:T(4,128)} %copy-done.13), calls=%async_computation.1 | async-start | bytes 8192 | tf_op jit(solution)/shard_map/slice | solution.py:420
  96.4 14.5 %copy-start.9 = (f32[512,1]{1,0:T(8,128)S(1)}, f32[512,1]{1,0:T(8,128)}, u32[]{:S(2)}) copy-start(f32[512,1]{1,0:T(8,128)} %copy-done.8) | copy-start | bytes 6148
  111.4 13.9 %copy-start.11 = (bf16[2,512,512]{2,1,0:T(8,128)(2,1)S(1)}, bf16[2,512,512]{2,1,0:T(8,128)(2,1)}, u32[]{:S(2)}) copy-start(bf16[2,512,512]{2,1,0:T(8,128)(2,1)} %slice.115) | copy-start | bytes 3145732
  111.5 13.9 %copy-start.12 = (bf16[1,512,512]{2,1,0:T(8,128)(2,1)S(1)}, bf16[1,512,512]{2,1,0:T(8,128)(2,1)}, u32[]{:S(2)}) copy-start(bf16[1,512,512]{2,1,0:T(8,128)(2,1)} %get-tuple-element.40) | copy-start | bytes 1572868
  125.4 1.2 copy-start.7
  125.5 19.7 %copy-start.1 = (f32[512,512]{1,0:T(8,128)S(1)}, f32[512,512]{1,0:T(8,128)}, u32[]{:S(2)}) copy-start(f32[512,512]{1,0:T(8,128)} %copy-done) | copy-start | bytes 3145732
  125.6 19.7 %copy-start.3 = (f32[512,512]{1,0:T(8,128)S(1)}, f32[512,512]{1,0:T(8,128)}, u32[]{:S(2)}) copy-start(f32[512,512]{1,0:T(8,128)} %copy-done.2) | copy-start | bytes 3145732
  125.6 19.7 %copy-start.5 = (f32[512,512]{1,0:T(8,128)S(1)}, f32[512,512]{1,0:T(8,128)}, u32[]{:S(2)}) copy-start(f32[512,512]{1,0:T(8,128)} %copy-done.4) | copy-start | bytes 3145732
  149.6 1.4 copy-start.14
  150.4 2.0 %collective-permute-start = (bf16[2,8,64,256]{3,2,1,0:T(8,128)(2,1)S(1)}, bf16[2,8,64,256]{3,2,1,0:T(8,128)(2,1)S(1)}, u32[]{:S(2)}, u32[]{:S(2)}) collective-permute-start(bf16[2,8,64,256]{3,2,1,0:T(8,128)(2,1)S(1)} %fusion.7), channel_id=1, source_target_pairs={{0,8},{8,0},{16,24},{24,16},{1,9},{9,1},{17,25},{25,17},{2,10},{10... | collective-permute-start | bytes 1572872 | tf_op jit(solution)/shard_map/ppermute | solution.py:384
  150.5 3.3 %collective-permute-start.5 = (bf16[2,8,64,256]{3,2,1,0:T(8,128)(2,1)S(1)}, bf16[2,8,64,256]{3,2,1,0:T(8,128)(2,1)S(1)}, u32[]{:S(2)}, u32[]{:S(2)}) collective-permute-start(bf16[2,8,64,256]{3,2,1,0:T(8,128)(2,1)S(1)} %fusion.8), channel_id=1, source_target_pairs={{0,8},{8,0},{16,24},{24,16},{1,9},{9,1},{17,25},{25,17},{2,10},{10... | collective-permute-start | bytes 1572872 | tf_op jit(solution)/shard_map/ppermute | solution.py:384
  152.5 8.4 %collective-permute-start.1 = (bf16[1,8,64,256]{3,2,1,0:T(8,128)(2,1)S(1)}, bf16[1,8,64,256]{3,2,1,0:T(8,128)(2,1)S(1)}, u32[]{:S(2)}, u32[]{:S(2)}) collective-permute-start(bf16[1,8,64,256]{3,2,1,0:T(8,128)(2,1)S(1)} %dynamic-slice_convert_fusion.3), channel_id=1, source_target_pairs={{0,16},{8,24},{16,0},{24,8},{1,17},{9,25},{17,1},{25,9},{2,18},{10... | collective-permute-start | bytes 786440 | tf_op jit(solution)/shard_map/ppermute | solution.py:384
  154.0 9.1 %collective-permute-start.6 = (bf16[2,4,64,256]{3,2,1,0:T(8,128)(2,1)S(1)}, bf16[2,4,64,256]{3,2,1,0:T(8,128)(2,1)S(1)}, u32[]{:S(2)}, u32[]{:S(2)}) collective-permute-start(bf16[2,4,64,256]{3,2,1,0:T(8,128)(2,1)S(1)} %fusion.10), channel_id=1, source_target_pairs={{0,1},{1,0},{2,3},{3,2},{4,5},{5,4},{6,7},{7,6},{8,9},{9,8},{10,11... | collective-permute-start | bytes 786440 | tf_op jit(solution)/shard_map/ppermute | solution.py:384
  161.0 5.0 %collective-permute-start.2 = (bf16[1,4,64,256]{3,2,1,0:T(8,128)(2,1)S(1)}, bf16[1,4,64,256]{3,2,1,0:T(8,128)(2,1)S(1)}, u32[]{:S(2)}, u32[]{:S(2)}) collective-permute-start(bf16[1,4,64,256]{3,2,1,0:T(8,128)(2,1)S(1)} %fusion.11), channel_id=1, source_target_pairs={{0,1},{1,0},{2,3},{3,2},{4,5},{5,4},{6,7},{7,6},{8,9},{9,8},{10,11... | collective-permute-start | bytes 393224 | tf_op jit(solution)/shard_map/ppermute | solution.py:384
  163.1 5.0 %collective-permute-start.7 = (bf16[1,4,64,256]{3,2,1,0:T(8,128)(2,1)S(1)}, bf16[1,4,64,256]{3,2,1,0:T(8,128)(2,1)S(1)}, u32[]{:S(2)}, u32[]{:S(2)}) collective-permute-start(bf16[1,4,64,256]{3,2,1,0:T(8,128)(2,1)S(1)} %dynamic-slice_convert_fusion.4), channel_id=1, source_target_pairs={{0,16},{8,24},{16,0},{24,8},{1,17},{9,25},{17,1},{25,9},{2,18},{10... | collective-permute-start | bytes 393224 | tf_op jit(solution)/shard_map/ppermute | solution.py:384
  166.1 4.3 %collective-permute-start.3 = (bf16[1,2,64,256]{3,2,1,0:T(8,128)(2,1)S(1)}, bf16[1,2,64,256]{3,2,1,0:T(8,128)(2,1)S(1)}, u32[]{:S(2)}, u32[]{:S(2)}) collective-permute-start(bf16[1,2,64,256]{3,2,1,0:T(8,128)(2,1)S(1)} %fusion.14), channel_id=1, source_target_pairs={{0,2},{1,3},{2,0},{3,1},{4,6},{5,7},{6,4},{7,5},{8,10},{9,11},{10,... | collective-permute-start | bytes 196616 | tf_op jit(solution)/shard_map/ppermute | solution.py:384
  168.2 4.4 %collective-permute-start.8 = (bf16[1,2,64,256]{3,2,1,0:T(8,128)(2,1)S(1)}, bf16[1,2,64,256]{3,2,1,0:T(8,128)(2,1)S(1)}, u32[]{:S(2)}, u32[]{:S(2)}) collective-permute-start(bf16[1,2,64,256]{3,2,1,0:T(8,128)(2,1)S(1)} %fusion.15), channel_id=1, source_target_pairs={{0,2},{1,3},{2,0},{3,1},{4,6},{5,7},{6,4},{7,5},{8,10},{9,11},{10,... | collective-permute-start | bytes 196616 | tf_op jit(solution)/shard_map/ppermute | solution.py:384
  170.5 4.9 %collective-permute-start.4 = (bf16[1,1,64,256]{3,2,1,0:T(8,128)(2,1)S(1)}, bf16[1,1,64,256]{3,2,1,0:T(8,128)(2,1)S(1)}, u32[]{:S(2)}, u32[]{:S(2)}) collective-permute-start(bf16[1,1,64,256]{3,2,1,0:T(8,128)(2,1)S(1)} %dynamic-slice_convert_fusion.8), channel_id=1, source_target_pairs={{0,4},{1,5},{2,6},{3,7},{4,0},{5,1},{6,2},{7,3},{8,12},{9,13},{10,... | collective-permute-start | bytes 98312 | tf_op jit(solution)/shard_map/ppermute | solution.py:384
  172.6 4.9 %collective-permute-start.9 = (bf16[1,1,64,256]{3,2,1,0:T(8,128)(2,1)S(1)}, bf16[1,1,64,256]{3,2,1,0:T(8,128)(2,1)S(1)}, u32[]{:S(2)}, u32[]{:S(2)}) collective-permute-start(bf16[1,1,64,256]{3,2,1,0:T(8,128)(2,1)S(1)} %dynamic-slice_convert_fusion.7), channel_id=1, source_target_pairs={{0,4},{1,5},{2,6},{3,7},{4,0},{5,1},{6,2},{7,3},{8,12},{9,13},{10,... | collective-permute-start | bytes 98312 | tf_op jit(solution)/shard_map/ppermute | solution.py:384
  (3 other events, 2.9 us)
Sparse Core Ops, SparseCore 0:
  11.4 25.1 all-gather.2

commit v4 on v3

--- a/solution.py
+++ b/solution.py
@@ -21,6 +21,85 @@
     values = features.astype(jnp.float32)
     scaled = values * lax.rsqrt(jnp.sum(values * values, axis=1, keepdims=True) + 1e-06)
     return scaled.astype(jnp.bfloat16)
+
+
+def gather_kernel(size, own_ref, all_ref, local_sem, send_sems, recv_sems):
+    me, place = lax.axis_index("sec"), lax.axis_index("proto")
+    core, line, lines = lax.rem(me, 2), me // 2, size // 2
+    half = lax.rem(place, 2)
+    rows = own_ref.shape[0] // 2
+    mine = pl.ds(pl.multiple_of(half * rows, 16), rows)
+    rest = pl.ds(pl.multiple_of((1 - half) * rows, 16), rows)
+    other_core = {"sec": me + 1 - 2 * core}
+    neighbour = {"proto": place + 1 - 2 * half}
+    across = [{"sec": lax.rem(line + k, lines) * 2 + core} for k in range(1, lines)]
+    source = [lax.rem(line - k + lines, lines) * 2 + core for k in range(1, lines)]
+    barrier = pltpu.get_barrier_semaphore()
+    for target in [other_core, neighbour] + across:
+        pl.semaphore_signal(
+            barrier, inc=1, device_id=target, device_id_type=pl.DeviceIdType.MESH
+        )
+    pl.semaphore_wait(barrier, lines + 1)
+
+    def copy_to(number, src, dst, target):
+        return pltpu.make_async_remote_copy(
+            src_ref=src,
+            dst_ref=dst,
+            send_sem=send_sems.at[number],
+            recv_sem=recv_sems.at[number],
+            device_id=target,
+            device_id_type=pl.DeviceIdType.MESH,
+        )
+
+    outer = [
+        copy_to(k, own_ref.at[mine], all_ref.at[me, mine], target)
+        for k, target in enumerate(across)
+    ]
+    for copy in outer:
+        copy.start()
+    whole = copy_to(4 * (lines - 1), own_ref, all_ref.at[me], other_core)
+    whole.start()
+    local = pltpu.make_async_copy(own_ref, all_ref.at[me], local_sem)
+    local.start()
+    sides, firsts, seconds = [], [], []
+    for k, block in enumerate(source):
+        outer[k].wait_recv()
+        piece = all_ref.at[block, mine]
+        side = copy_to(lines - 1 + k, piece, piece, neighbour)
+        first = copy_to(2 * (lines - 1) + k, piece, piece, other_core)
+        side.start()
+        first.start()
+        sides.append(side)
+        firsts.append(first)
+    for k, block in enumerate(source):
+        sides[k].wait_recv()
+        piece = all_ref.at[block, rest]
+        second = copy_to(3 * (lines - 1) + k, piece, piece, other_core)
+        second.start()
+        seconds.append(second)
+    local.wait()
+    whole.wait()
+    for copy in outer + sides:
+        copy.wait_send()
+    for copy in firsts + seconds:
+        copy.wait()
+
+
+def gather_rows(own, collective_id):
+    size = lax.axis_size("sec")
+    copies = 4 * (size // 2 - 1) + 1
+    return pl.pallas_call(
+        functools.partial(gather_kernel, size),
+        out_shape=jax.ShapeDtypeStruct((size,) + own.shape, own.dtype),
+        in_specs=[pl.BlockSpec(memory_space=pl.ANY)],
+        out_specs=pl.BlockSpec(memory_space=pl.ANY),
+        scratch_shapes=[
+            pltpu.SemaphoreType.DMA,
+            pltpu.SemaphoreType.DMA((copies,)),
+            pltpu.SemaphoreType.DMA((copies,)),
+        ],
+        compiler_params=pltpu.CompilerParams(collective_id=collective_id, has_side_effects=True),
+    )(own)
 
 
 def teacher_kernel(rows_ref_sec, rows_ref, proto_ref, expo_ref, top_ref):
@@ -409,9 +488,9 @@
     own_rows = unit_rows_of(features)
     sample = jnp.where(is_student, crop_sample, 0)
     digits = jnp.concatenate([sample // 128, sample % 128]).astype(jnp.bfloat16)
-    extra = -(-digits.shape[0] // (16 * width)) * 16
+    extra = -(-digits.shape[0] // (32 * width)) * 32
     digits = jnp.pad(digits, (0, extra * width - digits.shape[0])).reshape(extra, width)
-    packed = lax.all_gather(jnp.concatenate([own_rows, digits]), "sec", axis=0)
+    packed = gather_rows(jnp.concatenate([own_rows, digits]), ITERS + 1)
     all_rows = packed[:, :row_count]
     all_digits = packed[:, row_count:].reshape(sec_devs, -1)[:, : 2 * row_count].astype(jnp.int32)
     all_samples = all_digits[:, :row_count] * 128 + all_digits[:, row_count:]

time: 186 us -> 172 us (0.925)
  waiting for transfers between devices: 36.6 us -> 10.1 us
  Pallas kernels: 90.4 us -> 111 us
  between operations: 14.7 us -> 1.29 us
  local copies, waits for them, and re-layouts: 12.2 us -> 14.8 us
    all_gather x1 -> x0, waiting for transfers between devices: 25.1 us -> none  [per_device(): packed = lax.all_gather(jnp.concatenate([own_rows, digits]), 'sec', axis=0)]
    pallas_call x0 -> x1, Pallas kernels: none -> 21 us  [gather_rows(): pl.pallas_call(functools.partial(gather_kernel, size), out_shape=jax.Shap...]
    add x8, other arithmetic: 0.45 us -> 2.89 us  [halve(): blocks = keep + got.astype(jnp.float32)]
    unnamed x32 -> x34, local copies, waits for them, and re-layouts: 5.77 us -> 5.93 us
  transfers between devices with their start and end apart: 11 -> 10, of which waited for: 9 -> 9; matrix products, arithmetic and copies ran while one was open for 1% -> 2% of each run, Pallas kernels for 0% -> 0%
where the time goes in v4:
time: 172 us; the launch traced here: 171 us
  Pallas kernels  111 us (65%)
  other arithmetic  16 us (9%)
  local copies, waits for them, and re-layouts  14.8 us (9%)
  starting transfers between devices  14.6 us (8%)
  waiting for transfers between devices  10.1 us (6%)
  matrix products  2.81 us (2%)
    pallas_call x3, Pallas kernels, student_mean(): pl.pallas_call(functools.partial(student_kernel, steps, math.gcd(chunk, 1...  40.6 us
    pallas_call x1, Pallas kernels, gather_rows(): pl.pallas_call(functools.partial(gather_kernel, size), out_shape=jax.Shap...  21 us
    ppermute x10, starting transfers between devices, halve(): lax.ppermute(give.astype(jnp.bfloat16), axis, [(i, i ^ bit) for i in rang...  14.6 us
    pallas_call x2, Pallas kernels, sweep(): pl.pallas_call(functools.partial(sweep_kernel, protos), out_shape=jax.Sha...  14.1 us
    pallas_call x1, Pallas kernels, target_mean(): pl.pallas_call(functools.partial(mean_kernel, protos), out_shape=(jax.Sha...  12.8 us
    pallas_call x1, Pallas kernels, share(): pl.pallas_call(functools.partial(share_kernel, sizes, combine), out_shape...  12.7 us
    pallas_call x1, Pallas kernels, teacher_expo(): pl.pallas_call(teacher_kernel, out_shape=(jax.ShapeDtypeStruct((count, co...  10.3 us
    ppermute x10, waiting for transfers between devices, halve(): lax.ppermute(give.astype(jnp.bfloat16), axis, [(i, i ^ bit) for i in rang...  10.1 us
  transfers between devices with their start and end apart: 10, of which 9 were waited for; matrix products, arithmetic and copies ran while one was open for 2% of the time, Pallas kernels for 0%

profile of v4, /device:TPU:0, one launch (start us, length us, event | category | flops | bytes accessed | tf_op | source)
XLA Modules:
  0.0 171.1 jit_solution(11934112834575813764)
XLA Ops:
  4.7 21.0 %shard_map.59 = bf16[4,544,512]{2,1,0:T(8,128)(2,1)} custom-call(bf16[544,512]{1,0:T(8,128)(2,1)} %pad_maximum_fusion.2.own_ref), custom_call_target="tpu_custom_call" | custom-call | tf_op jit(solution)/shard_map/pallas_call | solution.py:91
  27.0 2.3 %slice.96 = bf16[2,512,512]{2,1,0:T(8,128)(2,1)} slice(bf16[4,544,512]{2,1,0:T(8,128)(2,1)} %shard_map.59), slice={[0:2], [0:512], [0:512]} | slice | bytes 2097152 | tf_op jit(solution)/shard_map/slice | solution.py:499
  30.3 10.3 %shard_map.60 = (bf16[512,8192]{1,0:T(8,128)(2,1)}, f32[4,512,1]{2,1,0:T(8,128)S(1)}) custom-call(s32[1]{0:T(128)} %bitcast.1.rows_ref_sec.sec_ref, bf16[512,512]{1,0:T(8,128)(2,1)S(1)} %get-tuple-element.43.rows_ref, bf16[512,32768]{1,0:T(8,128)(2,1)} %proto_ref.9), custom_call_target="tpu_custom_call" | custom-call | flops 4294967296 | bytes 16777216 | tf_op jit(solution)/shard_map/pallas_call | solution.py:123
  40.8 14.1 %shard_map.61 = (f32[512,512]{1,0:T(8,128)S(1)}, f32[512,1]{1,0:T(8,128)S(1)}, f32[512,1]{1,0:T(8,128)S(1)}, f32[8,128]{1,0:T(8,128)S(1)}) custom-call(bf16[512,512]{1,0:T(8,128)(2,1)S(1)} %get-tuple-element.44.rows_ref, f32[8,128]{1,0:T(8,128)S(1)} %pad_bitcast_fusion.6.value_ref, bf16[512,32768]{1,0:T(8,128)(2,1)} %proto_ref.9), custom_call_target="tpu_custom_call" | custom-call | flops 8589934592 | bytes 16777216 | tf_op jit(solution)/shard_map/pallas_call | solution.py:423
  56.3 7.0 %shard_map.62 = f32[512,1]{1,0:T(8,128)S(1)} custom-call(f32[4,512,1]{2,1,0:T(8,128)S(1)} %multiply_exponential_fusion.factor_ref, f32[512,1]{1,0:T(8,128)S(1)} %broadcast_7_weight_ref.2.weight_ref, bf16[512,8192]{1,0:T(8,128)(2,1)} %get-tuple-element.21.expo_ref), custom_call_target="tpu_custom_call" | custom-call | flops 25165824 | bytes 8388608 | tf_op jit(solution)/shard_map/pallas_call | solution.py:171
  63.4 13.3 %shard_map.63 = (f32[512,512]{1,0:T(8,128)S(1)}, f32[512,1]{1,0:T(8,128)S(1)}, f32[512,1]{1,0:T(8,128)S(1)}, f32[8,128]{1,0:T(8,128)S(1)}) custom-call(bf16[512,512]{1,0:T(8,128)(2,1)S(1)} %get-tuple-element.42.rows_ref, f32[8,128]{1,0:T(8,128)S(1)} %pad_bitcast_fusion.5.value_ref, bf16[512,32768]{1,0:T(8,128)(2,1)} %proto_ref.9), custom_call_target="tpu_custom_call" | custom-call | flops 8589934592 | bytes 16777216 | tf_op jit(solution)/shard_map/pallas_call | solution.py:423
  78.1 7.0 %shard_map.64 = f32[512,1]{1,0:T(8,128)S(1)} custom-call(f32[4,512,1]{2,1,0:T(8,128)S(1)} %multiply_exponential_fusion.factor_ref, f32[512,1]{1,0:T(8,128)S(1)} %copy.25.weight_ref, bf16[512,8192]{1,0:T(8,128)(2,1)} %get-tuple-element.21.expo_ref), custom_call_target="tpu_custom_call" | custom-call | flops 25165824 | bytes 8388608 | tf_op jit(solution)/shard_map/pallas_call | solution.py:171
  85.3 13.2 %shard_map.65 = (f32[512,512]{1,0:T(8,128)S(1)}, f32[512,1]{1,0:T(8,128)S(1)}, f32[512,1]{1,0:T(8,128)S(1)}, f32[8,128]{1,0:T(8,128)S(1)}) custom-call(bf16[512,512]{1,0:T(8,128)(2,1)S(1)} %get-tuple-element.41.rows_ref, f32[8,128]{1,0:T(8,128)S(1)} %pad_bitcast_fusion.4.value_ref, bf16[512,32768]{1,0:T(8,128)(2,1)} %proto_ref.9), custom_call_target="tpu_custom_call" | custom-call | flops 8589934592 | bytes 16777216 | tf_op jit(solution)/shard_map/pallas_call | solution.py:423
  100.5 12.8 %shard_map.66 = (f32[512,512]{1,0:T(8,128)S(1)}, f32[512,1]{1,0:T(8,128)S(1)}) custom-call(s32[1]{0:T(128)} %bitcast.1.rows_ref_sec.sec_ref, f32[4,512,1]{2,1,0:T(8,128)S(1)} %multiply_exponential_fusion.factor_ref, f32[512,1]{1,0:T(8,128)S(1)} %copy.32.weight_ref, bf16[512,8192]{1,0:T(8,128)(2,1)} %get-tuple-element.21.expo_ref, bf16[512,32768]{1,0:T(8,128)(2,1)} %proto_ref.9), custom_call_target="tpu_custom_call" | custom-call | flops 4294967296 | bytes 16777216 | tf_op jit(solution)/shard_map/pallas_call | solution.py:212
  115.6 2.8 %fusion.1 = (f32[1536]{0:T(1024)S(1)}, f32[1536,512]{1,0:T(8,128)}) fusion(bf16[3,512,512]{2,1,0:T(8,128)(2,1)S(1)} %pad_maximum_fusion.1, f32[512,512]{1,0:T(8,128)S(1)} %copy-done.7, s32[1536]{0:T(1024)S(1)} %eq.17), kind=kOutput, calls=%fused_computation.4 | convolution fusion | flops 808712704 | bytes 5779456 | tf_op jit(solution)/shard_map/dot_general | solution.py:527
  119.0 12.7 %shard_map.67 = f32[56,128]{1,0:T(8,128)} custom-call(f32[56,128]{1,0:T(8,128)} %pad_maximum_fusion.3.value_ref), custom_call_target="tpu_custom_call" | custom-call | tf_op jit(solution)/shard_map/pallas_call | solution.py:352
  133.9 3.3 %fusion = f32[1536,512]{1,0:T(8,128)S(1)} fusion(f32[512,512]{1,0:T(8,128)S(1)} %copy-done.5, f32[512,512]{1,0:T(8,128)S(1)} %copy-done.3, f32[512,512]{1,0:T(8,128)S(1)} %copy-done.1, f32[1536,512]{1,0:T(8,128)} %get-tuple-element.50, f32[1536]{0:T(1024)S(1)} %select_reduce_fusion, f32[1536]{0:T(1024)S(1)} %fusion.21), kind=kLoop, calls=%fused_computation.2 | loop fusion | flops 3932160 | bytes 9449472 | tf_op jit(solution)/shard_map/sub | solution.py:540
  138.3 1.9 %fusion.27 = (f32[4,8,64,256]{3,2,1,0:T(8,128)}, f32[4,8,64,256]{3,2,1,0:T(8,128)S(1)}) fusion(f32[4,8,64,512]{3,2,1,0:T(8,128)S(1)} %pad_maximum_fusion), kind=kLoop, calls=%fused_computation.99 | loop fusion | bytes 8388608 | tf_op jit(solution)/shard_map/slice | solution.py:546
  143.6 1.5 bitcast_add_fusion.1
  145.2 1.3 collective-permute-start.1
  147.7 1.8 %collective-permute-start.6 = (bf16[2,4,64,256]{3,2,1,0:T(8,128)(2,1)S(1)}, bf16[2,4,64,256]{3,2,1,0:T(8,128)(2,1)S(1)}, u32[]{:S(2)}, u32[]{:S(2)}) collective-permute-start(bf16[2,4,64,256]{3,2,1,0:T(8,128)(2,1)S(1)} %fusion.10), channel_id=1, source_target_pairs={{0,1},{1,0},{2,3},{3,2},{4,5},{5,4},{6,7},{7,6},{8,9},{9,8},{10,11... | collective-permute-start | bytes 786440 | tf_op jit(solution)/shard_map/ppermute | solution.py:463
  149.5 4.1 %collective-permute-done.1 = bf16[1,8,64,256]{3,2,1,0:T(8,128)(2,1)S(1)} collective-permute-done((bf16[1,8,64,256]{3,2,1,0:T(8,128)(2,1)S(1)}, bf16[1,8,64,256]{3,2,1,0:T(8,128)(2,1)S(1)}, u32[]{:S(2)}, u32[]{:S(2)}) %collective-permute-start.1) | collective-permute-done | bytes 262176 | tf_op jit(solution)/shard_map/ppermute | solution.py:463
  153.7 2.1 %collective-permute-start.2 = (bf16[1,4,64,256]{3,2,1,0:T(8,128)(2,1)S(1)}, bf16[1,4,64,256]{3,2,1,0:T(8,128)(2,1)S(1)}, u32[]{:S(2)}, u32[]{:S(2)}) collective-permute-start(bf16[1,4,64,256]{3,2,1,0:T(8,128)(2,1)S(1)} %fusion.11), channel_id=1, source_target_pairs={{0,1},{1,0},{2,3},{3,2},{4,5},{5,4},{6,7},{7,6},{8,9},{9,8},{10,11... | collective-permute-start | bytes 393224 | tf_op jit(solution)/shard_map/ppermute | solution.py:463
  157.0 1.7 collective-permute-done.2
  158.8 2.0 %collective-permute-start.3 = (bf16[1,2,64,256]{3,2,1,0:T(8,128)(2,1)S(1)}, bf16[1,2,64,256]{3,2,1,0:T(8,128)(2,1)S(1)}, u32[]{:S(2)}, u32[]{:S(2)}) collective-permute-start(bf16[1,2,64,256]{3,2,1,0:T(8,128)(2,1)S(1)} %fusion.14), channel_id=1, source_target_pairs={{0,2},{1,3},{2,0},{3,1},{4,6},{5,7},{6,4},{7,5},{8,10},{9,11},{10,... | collective-permute-start | bytes 196616 | tf_op jit(solution)/shard_map/ppermute | solution.py:463
  161.0 1.8 %collective-permute-start.8 = (bf16[1,2,64,256]{3,2,1,0:T(8,128)(2,1)S(1)}, bf16[1,2,64,256]{3,2,1,0:T(8,128)(2,1)S(1)}, u32[]{:S(2)}, u32[]{:S(2)}) collective-permute-start(bf16[1,2,64,256]{3,2,1,0:T(8,128)(2,1)S(1)} %fusion.15), channel_id=1, source_target_pairs={{0,2},{1,3},{2,0},{3,1},{4,6},{5,7},{6,4},{7,5},{8,10},{9,11},{10,... | collective-permute-start | bytes 196616 | tf_op jit(solution)/shard_map/ppermute | solution.py:463
  163.2 2.1 %collective-permute-start.4 = (bf16[1,1,64,256]{3,2,1,0:T(8,128)(2,1)S(1)}, bf16[1,1,64,256]{3,2,1,0:T(8,128)(2,1)S(1)}, u32[]{:S(2)}, u32[]{:S(2)}) collective-permute-start(bf16[1,1,64,256]{3,2,1,0:T(8,128)(2,1)S(1)} %dynamic-slice_convert_fusion.8), channel_id=1, source_target_pairs={{0,4},{1,5},{2,6},{3,7},{4,0},{5,1},{6,2},{7,3},{8,12},{9,13},{10,... | collective-permute-start | bytes 98312 | tf_op jit(solution)/shard_map/ppermute | solution.py:463
  165.4 1.9 %collective-permute-start.9 = (bf16[1,1,64,256]{3,2,1,0:T(8,128)(2,1)S(1)}, bf16[1,1,64,256]{3,2,1,0:T(8,128)(2,1)S(1)}, u32[]{:S(2)}, u32[]{:S(2)}) collective-permute-start(bf16[1,1,64,256]{3,2,1,0:T(8,128)(2,1)S(1)} %dynamic-slice_convert_fusion.7), channel_id=1, source_target_pairs={{0,4},{1,5},{2,6},{3,7},{4,0},{5,1},{6,2},{7,3},{8,12},{9,13},{10,... | collective-permute-start | bytes 98312 | tf_op jit(solution)/shard_map/ppermute | solution.py:463
  168.1 2.2 %collective-permute-done.9 = bf16[1,1,64,256]{3,2,1,0:T(8,128)(2,1)S(1)} collective-permute-done((bf16[1,1,64,256]{3,2,1,0:T(8,128)(2,1)S(1)}, bf16[1,1,64,256]{3,2,1,0:T(8,128)(2,1)S(1)}, u32[]{:S(2)}, u32[]{:S(2)}) %collective-permute-start.9) | collective-permute-done | bytes 32800 | tf_op jit(solution)/shard_map/ppermute | solution.py:463
  (123 shorter events, 25.6 us)
Async XLA Ops:
  25.7 3.5 %copy-start.10 = (bf16[4,544,512]{2,1,0:T(8,128)(2,1)S(1)}, bf16[4,544,512]{2,1,0:T(8,128)(2,1)}, u32[]{:S(2)}) copy-start(bf16[4,544,512]{2,1,0:T(8,128)(2,1)} %shard_map.59) | copy-start | bytes 6684676
  27.0 3.4 %copy-start.14 = (s32[4,512]{1,0:T(4,128)}, s32[4,512]{1,0:T(4,128)S(1)}, u32[]{:S(2)}) copy-start(s32[4,512]{1,0:T(4,128)S(1)} %slice_add_fusion) | copy-start | bytes 24580
  54.9 1.0 copy-start
  54.9 1.0 copy-start.8
  85.3 14.5 %slice-start = ((s32[4,512]{1,0:T(4,128)}), s32[2,512]{1,0:T(2,128)S(1)}, s32[]{:S(2)}) async-start(s32[4,512]{1,0:T(4,128)} %copy-done.14), calls=%async_computation | async-start | bytes 8192 | tf_op jit(solution)/shard_map/slice | solution.py:499
  85.3 14.5 %copy-start.9 = (f32[512,1]{1,0:T(8,128)S(1)}, f32[512,1]{1,0:T(8,128)}, u32[]{:S(2)}) copy-start(f32[512,1]{1,0:T(8,128)} %copy-done.8) | copy-start | bytes 6148
  100.4 13.9 %copy-start.11 = (bf16[2,512,512]{2,1,0:T(8,128)(2,1)S(1)}, bf16[2,512,512]{2,1,0:T(8,128)(2,1)}, u32[]{:S(2)}) copy-start(bf16[2,512,512]{2,1,0:T(8,128)(2,1)} %slice.96) | copy-start | bytes 3145732
  100.4 13.9 %copy-start.12 = (bf16[1,512,512]{2,1,0:T(8,128)(2,1)S(1)}, bf16[1,512,512]{2,1,0:T(8,128)(2,1)}, u32[]{:S(2)}) copy-start(bf16[1,512,512]{2,1,0:T(8,128)(2,1)} %get-tuple-element.40) | copy-start | bytes 1572868
  114.3 1.2 copy-start.7
  114.5 19.4 %copy-start.1 = (f32[512,512]{1,0:T(8,128)S(1)}, f32[512,512]{1,0:T(8,128)}, u32[]{:S(2)}) copy-start(f32[512,512]{1,0:T(8,128)} %copy-done) | copy-start | bytes 3145732
  114.5 19.4 %copy-start.3 = (f32[512,512]{1,0:T(8,128)S(1)}, f32[512,512]{1,0:T(8,128)}, u32[]{:S(2)}) copy-start(f32[512,512]{1,0:T(8,128)} %copy-done.2) | copy-start | bytes 3145732
  114.6 19.4 %copy-start.5 = (f32[512,512]{1,0:T(8,128)S(1)}, f32[512,512]{1,0:T(8,128)}, u32[]{:S(2)}) copy-start(f32[512,512]{1,0:T(8,128)} %copy-done.4) | copy-start | bytes 3145732
  138.3 3.9 %copy-start.13 = (f32[56,128]{1,0:T(8,128)S(1)}, f32[56,128]{1,0:T(8,128)}, u32[]{:S(2)}) copy-start(f32[56,128]{1,0:T(8,128)} %shard_map.67) | copy-start | bytes 86020
  138.3 4.0 %copy-start.15 = (s32[512]{0:T(512)S(1)}, s32[512]{0:T(512)}, u32[]{:S(2)}) copy-start(s32[512]{0:T(512)} %param.7) | copy-start | bytes 6148
  141.5 2.1 %collective-permute-start = (bf16[2,8,64,256]{3,2,1,0:T(8,128)(2,1)S(1)}, bf16[2,8,64,256]{3,2,1,0:T(8,128)(2,1)}, u32[]{:S(2)}, u32[]{:S(2)}) collective-permute-start(bf16[2,8,64,256]{3,2,1,0:T(8,128)(2,1)S(1)} %fusion.7), channel_id=1, source_target_pairs={{0,8},{8,0},{16,24},{24,16},{1,9},{9,1},{17,25},{25,17},{2,10},{10... | collective-permute-start | bytes 1572872 | tf_op jit(solution)/shard_map/ppermute | solution.py:463
  141.6 4.9 %collective-permute-start.5 = (bf16[2,8,64,256]{3,2,1,0:T(8,128)(2,1)S(1)}, bf16[2,8,64,256]{3,2,1,0:T(8,128)(2,1)}, u32[]{:S(2)}, u32[]{:S(2)}) collective-permute-start(bf16[2,8,64,256]{3,2,1,0:T(8,128)(2,1)S(1)} %fusion.8), channel_id=1, source_target_pairs={{0,8},{8,0},{16,24},{24,16},{1,9},{9,1},{17,25},{25,17},{2,10},{10... | collective-permute-start | bytes 1572872 | tf_op jit(solution)/shard_map/ppermute | solution.py:463
  145.2 8.4 %collective-permute-start.1 = (bf16[1,8,64,256]{3,2,1,0:T(8,128)(2,1)S(1)}, bf16[1,8,64,256]{3,2,1,0:T(8,128)(2,1)S(1)}, u32[]{:S(2)}, u32[]{:S(2)}) collective-permute-start(bf16[1,8,64,256]{3,2,1,0:T(8,128)(2,1)S(1)} %dynamic-slice_convert_fusion.3), channel_id=1, source_target_pairs={{0,16},{8,24},{16,0},{24,8},{1,17},{9,25},{17,1},{25,9},{2,18},{10... | collective-permute-start | bytes 786440 | tf_op jit(solution)/shard_map/ppermute | solution.py:463
  147.7 8.1 %collective-permute-start.6 = (bf16[2,4,64,256]{3,2,1,0:T(8,128)(2,1)S(1)}, bf16[2,4,64,256]{3,2,1,0:T(8,128)(2,1)S(1)}, u32[]{:S(2)}, u32[]{:S(2)}) collective-permute-start(bf16[2,4,64,256]{3,2,1,0:T(8,128)(2,1)S(1)} %fusion.10), channel_id=1, source_target_pairs={{0,1},{1,0},{2,3},{3,2},{4,5},{5,4},{6,7},{7,6},{8,9},{9,8},{10,11... | collective-permute-start | bytes 786440 | tf_op jit(solution)/shard_map/ppermute | solution.py:463
  153.7 5.0 %collective-permute-start.2 = (bf16[1,4,64,256]{3,2,1,0:T(8,128)(2,1)S(1)}, bf16[1,4,64,256]{3,2,1,0:T(8,128)(2,1)S(1)}, u32[]{:S(2)}, u32[]{:S(2)}) collective-permute-start(bf16[1,4,64,256]{3,2,1,0:T(8,128)(2,1)S(1)} %fusion.11), channel_id=1, source_target_pairs={{0,1},{1,0},{2,3},{3,2},{4,5},{5,4},{6,7},{7,6},{8,9},{9,8},{10,11... | collective-permute-start | bytes 393224 | tf_op jit(solution)/shard_map/ppermute | solution.py:463
  156.0 5.0 %collective-permute-start.7 = (bf16[1,4,64,256]{3,2,1,0:T(8,128)(2,1)S(1)}, bf16[1,4,64,256]{3,2,1,0:T(8,128)(2,1)S(1)}, u32[]{:S(2)}, u32[]{:S(2)}) collective-permute-start(bf16[1,4,64,256]{3,2,1,0:T(8,128)(2,1)S(1)} %dynamic-slice_convert_fusion.4), channel_id=1, source_target_pairs={{0,16},{8,24},{16,0},{24,8},{1,17},{9,25},{17,1},{25,9},{2,18},{10... | collective-permute-start | bytes 393224 | tf_op jit(solution)/shard_map/ppermute | solution.py:463
  158.8 4.3 %collective-permute-start.3 = (bf16[1,2,64,256]{3,2,1,0:T(8,128)(2,1)S(1)}, bf16[1,2,64,256]{3,2,1,0:T(8,128)(2,1)S(1)}, u32[]{:S(2)}, u32[]{:S(2)}) collective-permute-start(bf16[1,2,64,256]{3,2,1,0:T(8,128)(2,1)S(1)} %fusion.14), channel_id=1, source_target_pairs={{0,2},{1,3},{2,0},{3,1},{4,6},{5,7},{6,4},{7,5},{8,10},{9,11},{10,... | collective-permute-start | bytes 196616 | tf_op jit(solution)/shard_map/ppermute | solution.py:463
  161.0 4.3 %collective-permute-start.8 = (bf16[1,2,64,256]{3,2,1,0:T(8,128)(2,1)S(1)}, bf16[1,2,64,256]{3,2,1,0:T(8,128)(2,1)S(1)}, u32[]{:S(2)}, u32[]{:S(2)}) collective-permute-start(bf16[1,2,64,256]{3,2,1,0:T(8,128)(2,1)S(1)} %fusion.15), channel_id=1, source_target_pairs={{0,2},{1,3},{2,0},{3,1},{4,6},{5,7},{6,4},{7,5},{8,10},{9,11},{10,... | collective-permute-start | bytes 196616 | tf_op jit(solution)/shard_map/ppermute | solution.py:463
  163.2 4.9 %collective-permute-start.4 = (bf16[1,1,64,256]{3,2,1,0:T(8,128)(2,1)S(1)}, bf16[1,1,64,256]{3,2,1,0:T(8,128)(2,1)S(1)}, u32[]{:S(2)}, u32[]{:S(2)}) collective-permute-start(bf16[1,1,64,256]{3,2,1,0:T(8,128)(2,1)S(1)} %dynamic-slice_convert_fusion.8), channel_id=1, source_target_pairs={{0,4},{1,5},{2,6},{3,7},{4,0},{5,1},{6,2},{7,3},{8,12},{9,13},{10,... | collective-permute-start | bytes 98312 | tf_op jit(solution)/shard_map/ppermute | solution.py:463
  165.4 4.9 %collective-permute-start.9 = (bf16[1,1,64,256]{3,2,1,0:T(8,128)(2,1)S(1)}, bf16[1,1,64,256]{3,2,1,0:T(8,128)(2,1)S(1)}, u32[]{:S(2)}, u32[]{:S(2)}) collective-permute-start(bf16[1,1,64,256]{3,2,1,0:T(8,128)(2,1)S(1)} %dynamic-slice_convert_fusion.7), channel_id=1, source_target_pairs={{0,4},{1,5},{2,6},{3,7},{4,0},{5,1},{6,2},{7,3},{8,12},{9,13},{10,... | collective-permute-start | bytes 98312 | tf_op jit(solution)/shard_map/ppermute | solution.py:463
  (3 other events, 2.9 us)

commit v5 on v4

--- a/solution.py
+++ b/solution.py
@@ -194,15 +194,27 @@
         partial[...] = jnp.zeros_like(partial)
         mean_ref[...] = jnp.zeros_like(mean_ref)
 
-    expo = expo_ref[...].astype(jnp.float32) * factor_ref[0]
-    col_total = jnp.sum(expo * weight_ref[...], axis=0, keepdims=True)
-    col_scale = 1.0 / (protos * col_total)
-    target = (expo * col_scale).astype(jnp.bfloat16)
-    partial[...] += lanes_sum(target.astype(jnp.float32))
-    total_ref[...] = jnp.sum(partial[...], axis=1, keepdims=True)
-    mean_ref[...] += lax.dot_general(
-        target, proto_ref[...], (((1,), (1,)), ((), ())), preferred_element_type=jnp.float32
-    )
+    chunk = expo_ref.shape[1]
+    unit = math.gcd(chunk, 512)
+    row_part, mean_part = partial[...], mean_ref[...]
+    for at in range(0, chunk, unit):
+        expo = expo_ref[:, at : at + unit].astype(jnp.float32) * factor_ref[0]
+        col_total = jnp.sum(expo * weight_ref[...], axis=0, keepdims=True)
+        col_scale = 1.0 / (protos * col_total)
+        target = (expo * col_scale).astype(jnp.bfloat16)
+        row_part = row_part + lanes_sum(target.astype(jnp.float32))
+        mean_part = mean_part + lax.dot_general(
+            target,
+            proto_ref[:, at : at + unit],
+            (((1,), (1,)), ((), ())),
+            preferred_element_type=jnp.float32,
+        )
+    partial[...] = row_part
+    mean_ref[...] = mean_part
+
+    @pl.when(step == pl.num_programs(0) - 1)
+    def _():
+        total_ref[...] = jnp.sum(partial[...], axis=1, keepdims=True)
 
 
 def target_mean(sec_index, factor, weight, expo_tab, prototypes, protos, chunk):

time: 172 us -> 170 us (0.988)
  Pallas kernels: 111 us -> 109 us
    pallas_call x1, Pallas kernels: 12.8 us -> 10.5 us  [target_mean(): pl.pallas_call(functools.partial(mean_kernel, protos), out_shape=(jax.Sha...]
where the time goes in v5:
time: 170 us; the launch traced here: 169 us
  Pallas kernels  109 us (64%)
  other arithmetic  16 us (9%)
  local copies, waits for them, and re-layouts  14.8 us (9%)
  starting transfers between devices  14.6 us (9%)
  waiting for transfers between devices  10.1 us (6%)
  matrix products  2.81 us (2%)
    pallas_call x3, Pallas kernels, student_mean(): pl.pallas_call(functools.partial(student_kernel, steps, math.gcd(chunk, 1...  40.6 us
    pallas_call x1, Pallas kernels, gather_rows(): pl.pallas_call(functools.partial(gather_kernel, size), out_shape=jax.Shap...  21 us
    ppermute x10, starting transfers between devices, halve(): lax.ppermute(give.astype(jnp.bfloat16), axis, [(i, i ^ bit) for i in rang...  14.6 us
    pallas_call x2, Pallas kernels, sweep(): pl.pallas_call(functools.partial(sweep_kernel, protos), out_shape=jax.Sha...  14.1 us
    pallas_call x1, Pallas kernels, share(): pl.pallas_call(functools.partial(share_kernel, sizes, combine), out_shape...  12.7 us
    pallas_call x1, Pallas kernels, target_mean(): pl.pallas_call(functools.partial(mean_kernel, protos), out_shape=(jax.Sha...  10.5 us
    pallas_call x1, Pallas kernels, teacher_expo(): pl.pallas_call(teacher_kernel, out_shape=(jax.ShapeDtypeStruct((count, co...  10.3 us
    ppermute x10, waiting for transfers between devices, halve(): lax.ppermute(give.astype(jnp.bfloat16), axis, [(i, i ^ bit) for i in rang...  10.1 us
  transfers between devices with their start and end apart: 10, of which 9 were waited for; matrix products, arithmetic and copies ran while one was open for 2% of the time, Pallas kernels for 0%

profile of v5, /device:TPU:0, one launch (start us, length us, event | category | flops | bytes accessed | tf_op | source)
XLA Modules:
  0.0 168.8 jit_solution(15391901769113035760)
XLA Ops:
  4.7 21.0 %shard_map.59 = bf16[4,544,512]{2,1,0:T(8,128)(2,1)} custom-call(bf16[544,512]{1,0:T(8,128)(2,1)} %pad_maximum_fusion.2.own_ref), custom_call_target="tpu_custom_call" | custom-call | tf_op jit(solution)/shard_map/pallas_call | solution.py:91
  27.0 2.3 %slice.96 = bf16[2,512,512]{2,1,0:T(8,128)(2,1)} slice(bf16[4,544,512]{2,1,0:T(8,128)(2,1)} %shard_map.59), slice={[0:2], [0:512], [0:512]} | slice | bytes 2097152 | tf_op jit(solution)/shard_map/slice | solution.py:511
  30.3 10.3 %shard_map.60 = (bf16[512,8192]{1,0:T(8,128)(2,1)}, f32[4,512,1]{2,1,0:T(8,128)S(1)}) custom-call(s32[1]{0:T(128)} %bitcast.1.rows_ref_sec.sec_ref, bf16[512,512]{1,0:T(8,128)(2,1)S(1)} %get-tuple-element.43.rows_ref, bf16[512,32768]{1,0:T(8,128)(2,1)} %proto_ref.9), custom_call_target="tpu_custom_call" | custom-call | flops 4294967296 | bytes 16777216 | tf_op jit(solution)/shard_map/pallas_call | solution.py:123
  40.8 14.1 %shard_map.61 = (f32[512,512]{1,0:T(8,128)S(1)}, f32[512,1]{1,0:T(8,128)S(1)}, f32[512,1]{1,0:T(8,128)S(1)}, f32[8,128]{1,0:T(8,128)S(1)}) custom-call(bf16[512,512]{1,0:T(8,128)(2,1)S(1)} %get-tuple-element.44.rows_ref, f32[8,128]{1,0:T(8,128)S(1)} %pad_bitcast_fusion.6.value_ref, bf16[512,32768]{1,0:T(8,128)(2,1)} %proto_ref.9), custom_call_target="tpu_custom_call" | custom-call | flops 8589934592 | bytes 16777216 | tf_op jit(solution)/shard_map/pallas_call | solution.py:435
  56.3 7.0 %shard_map.62 = f32[512,1]{1,0:T(8,128)S(1)} custom-call(f32[4,512,1]{2,1,0:T(8,128)S(1)} %multiply_exponential_fusion.factor_ref, f32[512,1]{1,0:T(8,128)S(1)} %broadcast_7_weight_ref.2.weight_ref, bf16[512,8192]{1,0:T(8,128)(2,1)} %get-tuple-element.21.expo_ref), custom_call_target="tpu_custom_call" | custom-call | flops 25165824 | bytes 8388608 | tf_op jit(solution)/shard_map/pallas_call | solution.py:171
  63.4 13.3 %shard_map.63 = (f32[512,512]{1,0:T(8,128)S(1)}, f32[512,1]{1,0:T(8,128)S(1)}, f32[512,1]{1,0:T(8,128)S(1)}, f32[8,128]{1,0:T(8,128)S(1)}) custom-call(bf16[512,512]{1,0:T(8,128)(2,1)S(1)} %get-tuple-element.42.rows_ref, f32[8,128]{1,0:T(8,128)S(1)} %pad_bitcast_fusion.5.value_ref, bf16[512,32768]{1,0:T(8,128)(2,1)} %proto_ref.9), custom_call_target="tpu_custom_call" | custom-call | flops 8589934592 | bytes 16777216 | tf_op jit(solution)/shard_map/pallas_call | solution.py:435
  78.1 7.0 %shard_map.64 = f32[512,1]{1,0:T(8,128)S(1)} custom-call(f32[4,512,1]{2,1,0:T(8,128)S(1)} %multiply_exponential_fusion.factor_ref, f32[512,1]{1,0:T(8,128)S(1)} %copy.25.weight_ref, bf16[512,8192]{1,0:T(8,128)(2,1)} %get-tuple-element.21.expo_ref), custom_call_target="tpu_custom_call" | custom-call | flops 25165824 | bytes 8388608 | tf_op jit(solution)/shard_map/pallas_call | solution.py:171
  85.3 13.2 %shard_map.65 = (f32[512,512]{1,0:T(8,128)S(1)}, f32[512,1]{1,0:T(8,128)S(1)}, f32[512,1]{1,0:T(8,128)S(1)}, f32[8,128]{1,0:T(8,128)S(1)}) custom-call(bf16[512,512]{1,0:T(8,128)(2,1)S(1)} %get-tuple-element.41.rows_ref, f32[8,128]{1,0:T(8,128)S(1)} %pad_bitcast_fusion.4.value_ref, bf16[512,32768]{1,0:T(8,128)(2,1)} %proto_ref.9), custom_call_target="tpu_custom_call" | custom-call | flops 8589934592 | bytes 16777216 | tf_op jit(solution)/shard_map/pallas_call | solution.py:435
  100.5 10.5 %shard_map.66 = (f32[512,512]{1,0:T(8,128)S(1)}, f32[512,1]{1,0:T(8,128)S(1)}) custom-call(s32[1]{0:T(128)} %bitcast.1.rows_ref_sec.sec_ref, f32[4,512,1]{2,1,0:T(8,128)S(1)} %multiply_exponential_fusion.factor_ref, f32[512,1]{1,0:T(8,128)S(1)} %copy.32.weight_ref, bf16[512,8192]{1,0:T(8,128)(2,1)} %get-tuple-element.21.expo_ref, bf16[512,32768]{1,0:T(8,128)(2,1)} %proto_ref.9), custom_call_target="tpu_custom_call" | custom-call | flops 4294967296 | bytes 16777216 | tf_op jit(solution)/shard_map/pallas_call | solution.py:224
  113.3 2.8 %fusion.1 = (f32[1536]{0:T(1024)S(1)}, f32[1536,512]{1,0:T(8,128)}) fusion(bf16[3,512,512]{2,1,0:T(8,128)(2,1)S(1)} %pad_maximum_fusion.1, f32[512,512]{1,0:T(8,128)S(1)} %copy-done.7, s32[1536]{0:T(1024)S(1)} %eq.17), kind=kOutput, calls=%fused_computation.4 | convolution fusion | flops 808712704 | bytes 5779456 | tf_op jit(solution)/shard_map/dot_general | solution.py:539
  116.8 12.7 %shard_map.67 = f32[56,128]{1,0:T(8,128)} custom-call(f32[56,128]{1,0:T(8,128)} %pad_maximum_fusion.3.value_ref), custom_call_target="tpu_custom_call" | custom-call | tf_op jit(solution)/shard_map/pallas_call | solution.py:364
  131.7 3.3 %fusion = f32[1536,512]{1,0:T(8,128)S(1)} fusion(f32[512,512]{1,0:T(8,128)S(1)} %copy-done.5, f32[512,512]{1,0:T(8,128)S(1)} %copy-done.3, f32[512,512]{1,0:T(8,128)S(1)} %copy-done.1, f32[1536,512]{1,0:T(8,128)} %get-tuple-element.50, f32[1536]{0:T(1024)S(1)} %select_reduce_fusion, f32[1536]{0:T(1024)S(1)} %fusion.21), kind=kLoop, calls=%fused_computation.2 | loop fusion | flops 3932160 | bytes 9449472 | tf_op jit(solution)/shard_map/sub | solution.py:552
  136.1 1.9 %fusion.27 = (f32[4,8,64,256]{3,2,1,0:T(8,128)}, f32[4,8,64,256]{3,2,1,0:T(8,128)S(1)}) fusion(f32[4,8,64,512]{3,2,1,0:T(8,128)S(1)} %pad_maximum_fusion), kind=kLoop, calls=%fused_computation.99 | loop fusion | bytes 8388608 | tf_op jit(solution)/shard_map/slice | solution.py:558
  141.4 1.5 bitcast_add_fusion.1
  142.9 1.3 collective-permute-start.1
  145.5 1.8 %collective-permute-start.6 = (bf16[2,4,64,256]{3,2,1,0:T(8,128)(2,1)S(1)}, bf16[2,4,64,256]{3,2,1,0:T(8,128)(2,1)S(1)}, u32[]{:S(2)}, u32[]{:S(2)}) collective-permute-start(bf16[2,4,64,256]{3,2,1,0:T(8,128)(2,1)S(1)} %fusion.10), channel_id=1, source_target_pairs={{0,1},{1,0},{2,3},{3,2},{4,5},{5,4},{6,7},{7,6},{8,9},{9,8},{10,11... | collective-permute-start | bytes 786440 | tf_op jit(solution)/shard_map/ppermute | solution.py:475
  147.2 4.1 %collective-permute-done.1 = bf16[1,8,64,256]{3,2,1,0:T(8,128)(2,1)S(1)} collective-permute-done((bf16[1,8,64,256]{3,2,1,0:T(8,128)(2,1)S(1)}, bf16[1,8,64,256]{3,2,1,0:T(8,128)(2,1)S(1)}, u32[]{:S(2)}, u32[]{:S(2)}) %collective-permute-start.1) | collective-permute-done | bytes 262176 | tf_op jit(solution)/shard_map/ppermute | solution.py:475
  151.4 2.1 %collective-permute-start.2 = (bf16[1,4,64,256]{3,2,1,0:T(8,128)(2,1)S(1)}, bf16[1,4,64,256]{3,2,1,0:T(8,128)(2,1)S(1)}, u32[]{:S(2)}, u32[]{:S(2)}) collective-permute-start(bf16[1,4,64,256]{3,2,1,0:T(8,128)(2,1)S(1)} %fusion.11), channel_id=1, source_target_pairs={{0,1},{1,0},{2,3},{3,2},{4,5},{5,4},{6,7},{7,6},{8,9},{9,8},{10,11... | collective-permute-start | bytes 393224 | tf_op jit(solution)/shard_map/ppermute | solution.py:475
  154.8 1.7 collective-permute-done.2
  156.5 2.0 %collective-permute-start.3 = (bf16[1,2,64,256]{3,2,1,0:T(8,128)(2,1)S(1)}, bf16[1,2,64,256]{3,2,1,0:T(8,128)(2,1)S(1)}, u32[]{:S(2)}, u32[]{:S(2)}) collective-permute-start(bf16[1,2,64,256]{3,2,1,0:T(8,128)(2,1)S(1)} %fusion.14), channel_id=1, source_target_pairs={{0,2},{1,3},{2,0},{3,1},{4,6},{5,7},{6,4},{7,5},{8,10},{9,11},{10,... | collective-permute-start | bytes 196616 | tf_op jit(solution)/shard_map/ppermute | solution.py:475
  158.8 1.8 %collective-permute-start.8 = (bf16[1,2,64,256]{3,2,1,0:T(8,128)(2,1)S(1)}, bf16[1,2,64,256]{3,2,1,0:T(8,128)(2,1)S(1)}, u32[]{:S(2)}, u32[]{:S(2)}) collective-permute-start(bf16[1,2,64,256]{3,2,1,0:T(8,128)(2,1)S(1)} %fusion.15), channel_id=1, source_target_pairs={{0,2},{1,3},{2,0},{3,1},{4,6},{5,7},{6,4},{7,5},{8,10},{9,11},{10,... | collective-permute-start | bytes 196616 | tf_op jit(solution)/shard_map/ppermute | solution.py:475
  160.9 2.1 %collective-permute-start.4 = (bf16[1,1,64,256]{3,2,1,0:T(8,128)(2,1)S(1)}, bf16[1,1,64,256]{3,2,1,0:T(8,128)(2,1)S(1)}, u32[]{:S(2)}, u32[]{:S(2)}) collective-permute-start(bf16[1,1,64,256]{3,2,1,0:T(8,128)(2,1)S(1)} %dynamic-slice_convert_fusion.8), channel_id=1, source_target_pairs={{0,4},{1,5},{2,6},{3,7},{4,0},{5,1},{6,2},{7,3},{8,12},{9,13},{10,... | collective-permute-start | bytes 98312 | tf_op jit(solution)/shard_map/ppermute | solution.py:475
  163.2 1.9 %collective-permute-start.9 = (bf16[1,1,64,256]{3,2,1,0:T(8,128)(2,1)S(1)}, bf16[1,1,64,256]{3,2,1,0:T(8,128)(2,1)S(1)}, u32[]{:S(2)}, u32[]{:S(2)}) collective-permute-start(bf16[1,1,64,256]{3,2,1,0:T(8,128)(2,1)S(1)} %dynamic-slice_convert_fusion.7), channel_id=1, source_target_pairs={{0,4},{1,5},{2,6},{3,7},{4,0},{5,1},{6,2},{7,3},{8,12},{9,13},{10,... | collective-permute-start | bytes 98312 | tf_op jit(solution)/shard_map/ppermute | solution.py:475
  165.8 2.2 %collective-permute-done.9 = bf16[1,1,64,256]{3,2,1,0:T(8,128)(2,1)S(1)} collective-permute-done((bf16[1,1,64,256]{3,2,1,0:T(8,128)(2,1)S(1)}, bf16[1,1,64,256]{3,2,1,0:T(8,128)(2,1)S(1)}, u32[]{:S(2)}, u32[]{:S(2)}) %collective-permute-start.9) | collective-permute-done | bytes 32800 | tf_op jit(solution)/shard_map/ppermute | solution.py:475
  (123 shorter events, 25.6 us)
Async XLA Ops:
  25.7 3.5 %copy-start.10 = (bf16[4,544,512]{2,1,0:T(8,128)(2,1)S(1)}, bf16[4,544,512]{2,1,0:T(8,128)(2,1)}, u32[]{:S(2)}) copy-start(bf16[4,544,512]{2,1,0:T(8,128)(2,1)} %shard_map.59) | copy-start | bytes 6684676
  27.0 3.4 %copy-start.14 = (s32[4,512]{1,0:T(4,128)}, s32[4,512]{1,0:T(4,128)S(1)}, u32[]{:S(2)}) copy-start(s32[4,512]{1,0:T(4,128)S(1)} %slice_add_fusion) | copy-start | bytes 24580
  54.9 1.0 copy-start
  54.9 1.0 copy-start.8
  85.3 14.5 %slice-start = ((s32[4,512]{1,0:T(4,128)}), s32[2,512]{1,0:T(2,128)S(1)}, s32[]{:S(2)}) async-start(s32[4,512]{1,0:T(4,128)} %copy-done.14), calls=%async_computation | async-start | bytes 8192 | tf_op jit(solution)/shard_map/slice | solution.py:511
  85.3 14.5 %copy-start.9 = (f32[512,1]{1,0:T(8,128)S(1)}, f32[512,1]{1,0:T(8,128)}, u32[]{:S(2)}) copy-start(f32[512,1]{1,0:T(8,128)} %copy-done.8) | copy-start | bytes 6148
  100.4 11.7 %copy-start.11 = (bf16[2,512,512]{2,1,0:T(8,128)(2,1)S(1)}, bf16[2,512,512]{2,1,0:T(8,128)(2,1)}, u32[]{:S(2)}) copy-start(bf16[2,512,512]{2,1,0:T(8,128)(2,1)} %slice.96) | copy-start | bytes 3145732
  100.4 11.7 %copy-start.12 = (bf16[1,512,512]{2,1,0:T(8,128)(2,1)S(1)}, bf16[1,512,512]{2,1,0:T(8,128)(2,1)}, u32[]{:S(2)}) copy-start(bf16[1,512,512]{2,1,0:T(8,128)(2,1)} %get-tuple-element.40) | copy-start | bytes 1572868
  112.1 1.2 copy-start.7
  112.3 19.4 %copy-start.1 = (f32[512,512]{1,0:T(8,128)S(1)}, f32[512,512]{1,0:T(8,128)}, u32[]{:S(2)}) copy-start(f32[512,512]{1,0:T(8,128)} %copy-done) | copy-start | bytes 3145732
  112.3 19.4 %copy-start.3 = (f32[512,512]{1,0:T(8,128)S(1)}, f32[512,512]{1,0:T(8,128)}, u32[]{:S(2)}) copy-start(f32[512,512]{1,0:T(8,128)} %copy-done.2) | copy-start | bytes 3145732
  112.3 19.4 %copy-start.5 = (f32[512,512]{1,0:T(8,128)S(1)}, f32[512,512]{1,0:T(8,128)}, u32[]{:S(2)}) copy-start(f32[512,512]{1,0:T(8,128)} %copy-done.4) | copy-start | bytes 3145732
  136.1 3.9 %copy-start.13 = (f32[56,128]{1,0:T(8,128)S(1)}, f32[56,128]{1,0:T(8,128)}, u32[]{:S(2)}) copy-start(f32[56,128]{1,0:T(8,128)} %shard_map.67) | copy-start | bytes 86020
  136.1 4.0 %copy-start.15 = (s32[512]{0:T(512)S(1)}, s32[512]{0:T(512)}, u32[]{:S(2)}) copy-start(s32[512]{0:T(512)} %param.7) | copy-start | bytes 6148
  139.3 2.1 %collective-permute-start = (bf16[2,8,64,256]{3,2,1,0:T(8,128)(2,1)S(1)}, bf16[2,8,64,256]{3,2,1,0:T(8,128)(2,1)}, u32[]{:S(2)}, u32[]{:S(2)}) collective-permute-start(bf16[2,8,64,256]{3,2,1,0:T(8,128)(2,1)S(1)} %fusion.7), channel_id=1, source_target_pairs={{0,8},{8,0},{16,24},{24,16},{1,9},{9,1},{17,25},{25,17},{2,10},{10... | collective-permute-start | bytes 1572872 | tf_op jit(solution)/shard_map/ppermute | solution.py:475
  139.4 4.9 %collective-permute-start.5 = (bf16[2,8,64,256]{3,2,1,0:T(8,128)(2,1)S(1)}, bf16[2,8,64,256]{3,2,1,0:T(8,128)(2,1)}, u32[]{:S(2)}, u32[]{:S(2)}) collective-permute-start(bf16[2,8,64,256]{3,2,1,0:T(8,128)(2,1)S(1)} %fusion.8), channel_id=1, source_target_pairs={{0,8},{8,0},{16,24},{24,16},{1,9},{9,1},{17,25},{25,17},{2,10},{10... | collective-permute-start | bytes 1572872 | tf_op jit(solution)/shard_map/ppermute | solution.py:475
  142.9 8.4 %collective-permute-start.1 = (bf16[1,8,64,256]{3,2,1,0:T(8,128)(2,1)S(1)}, bf16[1,8,64,256]{3,2,1,0:T(8,128)(2,1)S(1)}, u32[]{:S(2)}, u32[]{:S(2)}) collective-permute-start(bf16[1,8,64,256]{3,2,1,0:T(8,128)(2,1)S(1)} %dynamic-slice_convert_fusion.3), channel_id=1, source_target_pairs={{0,16},{8,24},{16,0},{24,8},{1,17},{9,25},{17,1},{25,9},{2,18},{10... | collective-permute-start | bytes 786440 | tf_op jit(solution)/shard_map/ppermute | solution.py:475
  145.5 8.1 %collective-permute-start.6 = (bf16[2,4,64,256]{3,2,1,0:T(8,128)(2,1)S(1)}, bf16[2,4,64,256]{3,2,1,0:T(8,128)(2,1)S(1)}, u32[]{:S(2)}, u32[]{:S(2)}) collective-permute-start(bf16[2,4,64,256]{3,2,1,0:T(8,128)(2,1)S(1)} %fusion.10), channel_id=1, source_target_pairs={{0,1},{1,0},{2,3},{3,2},{4,5},{5,4},{6,7},{7,6},{8,9},{9,8},{10,11... | collective-permute-start | bytes 786440 | tf_op jit(solution)/shard_map/ppermute | solution.py:475
  151.4 5.0 %collective-permute-start.2 = (bf16[1,4,64,256]{3,2,1,0:T(8,128)(2,1)S(1)}, bf16[1,4,64,256]{3,2,1,0:T(8,128)(2,1)S(1)}, u32[]{:S(2)}, u32[]{:S(2)}) collective-permute-start(bf16[1,4,64,256]{3,2,1,0:T(8,128)(2,1)S(1)} %fusion.11), channel_id=1, source_target_pairs={{0,1},{1,0},{2,3},{3,2},{4,5},{5,4},{6,7},{7,6},{8,9},{9,8},{10,11... | collective-permute-start | bytes 393224 | tf_op jit(solution)/shard_map/ppermute | solution.py:475
  153.7 5.0 %collective-permute-start.7 = (bf16[1,4,64,256]{3,2,1,0:T(8,128)(2,1)S(1)}, bf16[1,4,64,256]{3,2,1,0:T(8,128)(2,1)S(1)}, u32[]{:S(2)}, u32[]{:S(2)}) collective-permute-start(bf16[1,4,64,256]{3,2,1,0:T(8,128)(2,1)S(1)} %dynamic-slice_convert_fusion.4), channel_id=1, source_target_pairs={{0,16},{8,24},{16,0},{24,8},{1,17},{9,25},{17,1},{25,9},{2,18},{10... | collective-permute-start | bytes 393224 | tf_op jit(solution)/shard_map/ppermute | solution.py:475
  156.5 4.3 %collective-permute-start.3 = (bf16[1,2,64,256]{3,2,1,0:T(8,128)(2,1)S(1)}, bf16[1,2,64,256]{3,2,1,0:T(8,128)(2,1)S(1)}, u32[]{:S(2)}, u32[]{:S(2)}) collective-permute-start(bf16[1,2,64,256]{3,2,1,0:T(8,128)(2,1)S(1)} %fusion.14), channel_id=1, source_target_pairs={{0,2},{1,3},{2,0},{3,1},{4,6},{5,7},{6,4},{7,5},{8,10},{9,11},{10,... | collective-permute-start | bytes 196616 | tf_op jit(solution)/shard_map/ppermute | solution.py:475
  158.8 4.3 %collective-permute-start.8 = (bf16[1,2,64,256]{3,2,1,0:T(8,128)(2,1)S(1)}, bf16[1,2,64,256]{3,2,1,0:T(8,128)(2,1)S(1)}, u32[]{:S(2)}, u32[]{:S(2)}) collective-permute-start(bf16[1,2,64,256]{3,2,1,0:T(8,128)(2,1)S(1)} %fusion.15), channel_id=1, source_target_pairs={{0,2},{1,3},{2,0},{3,1},{4,6},{5,7},{6,4},{7,5},{8,10},{9,11},{10,... | collective-permute-start | bytes 196616 | tf_op jit(solution)/shard_map/ppermute | solution.py:475
  160.9 4.9 %collective-permute-start.4 = (bf16[1,1,64,256]{3,2,1,0:T(8,128)(2,1)S(1)}, bf16[1,1,64,256]{3,2,1,0:T(8,128)(2,1)S(1)}, u32[]{:S(2)}, u32[]{:S(2)}) collective-permute-start(bf16[1,1,64,256]{3,2,1,0:T(8,128)(2,1)S(1)} %dynamic-slice_convert_fusion.8), channel_id=1, source_target_pairs={{0,4},{1,5},{2,6},{3,7},{4,0},{5,1},{6,2},{7,3},{8,12},{9,13},{10,... | collective-permute-start | bytes 98312 | tf_op jit(solution)/shard_map/ppermute | solution.py:475
  163.2 4.9 %collective-permute-start.9 = (bf16[1,1,64,256]{3,2,1,0:T(8,128)(2,1)S(1)}, bf16[1,1,64,256]{3,2,1,0:T(8,128)(2,1)S(1)}, u32[]{:S(2)}, u32[]{:S(2)}) collective-permute-start(bf16[1,1,64,256]{3,2,1,0:T(8,128)(2,1)S(1)} %dynamic-slice_convert_fusion.7), channel_id=1, source_target_pairs={{0,4},{1,5},{2,6},{3,7},{4,0},{5,1},{6,2},{7,3},{8,12},{9,13},{10,... | collective-permute-start | bytes 98312 | tf_op jit(solution)/shard_map/ppermute | solution.py:475
  (3 other events, 2.9 us)
